TPU v7x, 512 devices: a whole 4x8x8 slice. The times are simulated.
512 devices in a mesh: ctx: 64 (over x, z, core), head: 8 (over y).
Axes of the slice: x: 4, y: 8, z: 8, core: 2. Of those that a mesh axis runs over, the one named last changes fastest.
Arguments:
- lin_query: bfloat16 [8192, 32, 128], P('ctx', 'head'), may hold values from -6 to 6
- lin_keys: bfloat16 [8192, 32, 128], P('ctx', 'head'), may hold values from -1.5 to 1.5
- lin_values: bfloat16 [8192, 32, 128], P('ctx', 'head'), may hold values from -6 to 6
- log_decay: float32 [32, 8192], P('head', 'ctx'), may hold values from -1 to 0
- norm_gain: float32 [32, 128], P('head'), may hold values from 0.1 to 1.9
- lin_cotangent: bfloat16 [8192, 32, 128], P('ctx', 'head'), may hold values from -6 to 6
- soft_query: bfloat16 [8192, 32, 128], P('ctx', 'head'), may hold values from -6 to 6
- soft_keys: bfloat16 [8192, 32, 128], P('ctx', 'head'), may hold values from -6 to 6
- soft_values: bfloat16 [8192, 32, 128], P('ctx', 'head'), may hold values from -6 to 6
- soft_cotangent: bfloat16 [8192, 32, 128], P('ctx', 'head'), may hold values from -6 to 6
- doc_start: int32 [8192], P('ctx'), may hold values from 0 to 8191, as said below
Outputs:
- lin_output: bfloat16 [8192, 32, 128], P('ctx', 'head')
- lin_query_grad: bfloat16 [8192, 32, 128], P('ctx', 'head')
- lin_key_grad: bfloat16 [8192, 32, 128], P('ctx', 'head')
- lin_value_grad: bfloat16 [8192, 32, 128], P('ctx', 'head')
- soft_output: bfloat16 [8192, 32, 128], P('ctx', 'head')
- soft_query_grad: bfloat16 [8192, 32, 128], P('ctx', 'head')
- soft_key_grad: bfloat16 [8192, 32, 128], P('ctx', 'head')
- soft_value_grad: bfloat16 [8192, 32, 128], P('ctx', 'head')
Inputs may be any that keep to these rules, and one draw needn't show every extreme that they name: doc_start[t] is where token t's document begins: it never falls, equals t or doc_start[t - 1], and t - doc_start[t] < 512; every draw holds a document of exactly 512 tokens, and the last token begins a document of its own.
All inputs are finite; a program needn't handle non-finite values.
Results may differ from a plain program's by a relative error of at most 0.03.
Values may be sent and summed in bfloat16 or wider, within the bound.
A program may use at most 128 MiB of HBM per device.

v0:
```python
import math

import jax
import jax.numpy as jnp
from jax import lax
from jax.sharding import PartitionSpec as P

SPAN = 4


norm_eps = 1e-05


def from_behind(value, axis, steps):
    count = lax.axis_size(axis)
    initial, last = (max(0, -steps), min(count, count - steps))
    return lax.ppermute(value, axis, [(source, source + steps) for source in range(initial, last)])


def local_masks(decays, starts, first_row):
    tok_rows = starts.shape[0]
    cumulative = jnp.cumsum(decays, axis=1)
    position = jnp.arange(tok_rows, dtype=jnp.int32)
    same_doc = (starts[:, None] == starts[None, :]) & (position[None, :] <= position[:, None])
    log_gap = jnp.minimum(cumulative[:, :, None] - cumulative[:, None, :], 0.0)
    within = jnp.where(same_doc[None], jnp.exp(log_gap), 0.0)
    entering = jnp.where((starts < first_row)[None, :], jnp.exp(cumulative), 0.0)
    leaving = jnp.where(
        (starts == starts[tok_rows - 1])[None, :],
        jnp.exp(cumulative[:, tok_rows - 1 :] - cumulative),
        0.0,
    )
    return (within, entering, leaving)


def shards(
    lin_query,
    lin_keys,
    lin_values,
    log_decay,
    norm_gain,
    lin_cotangent,
    soft_query,
    soft_keys,
    soft_values,
    soft_cotangent,
    doc_start,
):
    tok_rows = lin_query.shape[0]
    head_count = lin_query.shape[1]
    head_size = lin_query.shape[2]
    first_row = lax.axis_index("ctx") * tok_rows
    within, entering, leaving = local_masks(log_decay, doc_start, first_row)
    enter_rows = jnp.transpose(entering)[:, :, None]
    leave_rows = jnp.transpose(leaving)[:, :, None]
    passing = entering[:, tok_rows - 1]
    keyed_rows = (leave_rows * lin_keys).astype(jnp.bfloat16)
    closing = jnp.einsum("shd,she->hde", keyed_rows, lin_values, preferred_element_type=jnp.float32)
    incoming = jnp.zeros_like(closing)
    for step in range(SPAN):
        incoming = from_behind(passing[:, None, None] * incoming + closing, "ctx", 1)
    state_low = incoming.astype(jnp.bfloat16)
    scores = jnp.einsum("thd,shd->hts", lin_query, lin_keys, preferred_element_type=jnp.float32)
    attend = (within * scores).astype(jnp.bfloat16)
    intra = jnp.einsum("hts,she->the", attend, lin_values, preferred_element_type=jnp.float32)
    inter = jnp.einsum("thd,hde->the", lin_query, state_low, preferred_element_type=jnp.float32)
    raw_out = intra + enter_rows * inter
    gained = lin_cotangent.astype(jnp.float32) * norm_gain[None]
    squares, crossed = lax.psum(
        (jnp.sum(raw_out * raw_out, axis=(1, 2)), jnp.sum(gained * raw_out, axis=(1, 2))), "head"
    )
    feat_count = head_count * head_size * lax.axis_size("head")
    rscale = lax.rsqrt(squares / feat_count + norm_eps)[:, None, None]
    lin_output = (raw_out * rscale * norm_gain[None]).astype(jnp.bfloat16)
    raw_grad = (
        rscale * gained - raw_out * rscale**3 * (crossed[:, None, None] / feat_count)
    ).astype(jnp.bfloat16)
    carried = (enter_rows * lin_query).astype(jnp.bfloat16)
    pulled = jnp.einsum("thd,the->hde", carried, raw_grad, preferred_element_type=jnp.float32)
    outgoing = jnp.zeros_like(pulled)
    for step in range(SPAN):
        outgoing = from_behind(pulled + passing[:, None, None] * outgoing, "ctx", -1)
    back_low = outgoing.astype(jnp.bfloat16)
    pushes = jnp.einsum("the,she->hts", raw_grad, lin_values, preferred_element_type=jnp.float32)
    mixed = (within * pushes).astype(jnp.bfloat16)
    lin_query_grad = (
        jnp.einsum("hts,shd->thd", mixed, lin_keys, preferred_element_type=jnp.float32)
        + enter_rows
        * jnp.einsum("the,hde->thd", raw_grad, state_low, preferred_element_type=jnp.float32)
    ).astype(jnp.bfloat16)
    lin_key_grad = (
        jnp.einsum("hts,thd->shd", mixed, lin_query, preferred_element_type=jnp.float32)
        + leave_rows
        * jnp.einsum("she,hde->shd", lin_values, back_low, preferred_element_type=jnp.float32)
    ).astype(jnp.bfloat16)
    lin_value_grad = (
        jnp.einsum("hts,the->she", attend, raw_grad, preferred_element_type=jnp.float32)
        + leave_rows
        * jnp.einsum("shd,hde->she", lin_keys, back_low, preferred_element_type=jnp.float32)
    ).astype(jnp.bfloat16)
    inv_root = 1.0 / math.sqrt(head_size)
    stacked = jnp.stack([soft_keys, soft_values])
    blocks = [stacked]
    for step in range(SPAN):
        stacked = from_behind(stacked, "ctx", 1)
        blocks.append(stacked)
    ordered = blocks[::-1]
    window = jnp.concatenate(ordered, axis=1)
    window_keys = window[0]
    window_values = window[1]
    span_rows = SPAN * tok_rows
    width_rows = span_rows + tok_rows
    key_pos = first_row - span_rows + jnp.arange(width_rows, dtype=jnp.int32)
    query_pos = first_row + jnp.arange(tok_rows, dtype=jnp.int32)
    allowed = (key_pos[None, :] <= query_pos[:, None]) & (key_pos[None, :] >= doc_start[:, None])
    logits = jnp.einsum("thd,shd->hts", soft_query, window_keys, preferred_element_type=jnp.float32)
    logits = jnp.where(allowed[None], logits * inv_root, -jnp.inf)
    row_top = jnp.max(logits, axis=2, keepdims=True)
    expo = jnp.exp(logits - row_top)
    row_total = jnp.sum(expo, axis=2, keepdims=True)
    log_total = row_top + jnp.log(row_total)
    soft_output = (
        jnp.einsum(
            "hts,she->the",
            expo.astype(jnp.bfloat16),
            window_values,
            preferred_element_type=jnp.float32,
        )
        / jnp.transpose(row_total, (1, 0, 2))
    ).astype(jnp.bfloat16)
    row_delta = jnp.sum(
        soft_cotangent.astype(jnp.float32) * soft_output.astype(jnp.float32), axis=2
    )
    probs = jnp.exp(logits - log_total)
    cot_dots = jnp.einsum(
        "the,she->hts", soft_cotangent, window_values, preferred_element_type=jnp.float32
    )
    slopes = (inv_root * probs * (cot_dots - jnp.transpose(row_delta)[:, :, None])).astype(
        jnp.bfloat16
    )
    soft_query_grad = jnp.einsum(
        "hts,shd->thd", slopes, window_keys, preferred_element_type=jnp.float32
    ).astype(jnp.bfloat16)
    prob_low = probs.astype(jnp.bfloat16)
    key_part = jnp.einsum("hts,thd->shd", slopes, soft_query, preferred_element_type=jnp.float32)
    value_part = jnp.einsum(
        "hts,the->she", prob_low, soft_cotangent, preferred_element_type=jnp.float32
    )
    stacked_grads = jnp.stack([key_part, value_part])
    returning = stacked_grads[:, :tok_rows]
    for step in range(1, SPAN + 1):
        returning = (
            from_behind(returning, "ctx", -1)
            + stacked_grads[:, step * tok_rows : (step + 1) * tok_rows]
        )
    soft_key_grad = returning[0].astype(jnp.bfloat16)
    soft_value_grad = returning[1].astype(jnp.bfloat16)
    return (
        lin_output,
        lin_query_grad,
        lin_key_grad,
        lin_value_grad,
        soft_output,
        soft_query_grad,
        soft_key_grad,
        soft_value_grad,
    )


def solution(mesh):
    in_specs = (
        P("ctx", "head", None),
        P("ctx", "head", None),
        P("ctx", "head", None),
        P("head", "ctx"),
        P("head", None),
        P("ctx", "head", None),
        P("ctx", "head", None),
        P("ctx", "head", None),
        P("ctx", "head", None),
        P("ctx", "head", None),
        P("ctx"),
    )
    out_specs = (
        P("ctx", "head", None),
        P("ctx", "head", None),
        P("ctx", "head", None),
        P("ctx", "head", None),
        P("ctx", "head", None),
        P("ctx", "head", None),
        P("ctx", "head", None),
        P("ctx", "head", None),
    )
    return jax.shard_map(shards, mesh=mesh, in_specs=in_specs, out_specs=out_specs, check_vma=False)
```

profile of v0, /device:TPU:7, one launch (start us, length us, event | category | flops | bytes accessed | tf_op | source)
XLA Modules:
  0.0 131.5 jit_solution(6863087667989462305)
XLA Ops:
  0.7 1.3 slice.39
  2.0 1.0 reduce_window_sum.11
  2.9 0.2 slice_reduce_fusion
  3.1 1.3 broadcast_compare_fusion
  4.5 0.2 slice_reduce_fusion.1
  4.7 1.3 %broadcast_add_fusion.1 = (f32[4,128,128]{2,1,0:T(8,128)S(1)}, f32[4,128,128]{2,1,0:T(8,128)S(1)}) fusion(f32[4]{0:T(128)S(1)} %broadcast_multiply_fusion.1, bf16[128,4,128]{2,1,0:T(4,128)(2,1)} %param.13, f32[128,4]{0,1:T(4,128)S(1)} %get-tuple-element.32, bf16[128,4,128]{2,1,0:T(4,128)(2,1)} %param.12), kind=kOutput, calls=%fused_computation.89 | convolution fusion | flops 17039360 | bytes 788496 | tf_op jit(solution)/shard_map/shd,she->hde/dot_general | solution.py:58
  6.1 4.6 %collective-permute-start = (f32[4,128,128]{2,1,0:T(8,128)S(1)}, f32[4,128,128]{2,1,0:T(8,128)S(1)}, u32[]{:S(2)}, u32[]{:S(2)}) collective-permute-start(f32[4,128,128]{2,1,0:T(8,128)S(1)} %get-tuple-element.38), channel_id=1, source_target_pairs={{0,8},{8,16},{16,24},{24,32},{32,40},{40,48},{48,56},{56,64},{64,7... | collective-permute-start | bytes 786440 | tf_op jit(solution)/shard_map/ppermute | solution.py:17
  10.6 1.0 copy_bitcast_fusion
  11.7 2.1 %collective-permute-start.8 = (bf16[2,128,4,128]{3,1,2,0:T(8,128)(2,1)S(1)}, bf16[2,128,4,128]{3,1,2,0:T(8,128)(2,1)S(1)}, u32[]{:S(2)}, u32[]{:S(2)}) collective-permute-start(bf16[2,128,4,128]{3,1,2,0:T(8,128)(2,1)S(1)} %pad_maximum_fusion.1), channel_id=1, source_target_pairs={{0,8},{8,16},{16,24},{24,32},{32,40},{40,48},{48,56},{56,64},{64,7... | collective-permute-start | bytes 786440 | tf_op jit(solution)/shard_map/ppermute | solution.py:17
  14.1 4.5 %collective-permute-start.1 = (f32[4,128,128]{2,1,0:T(8,128)S(1)}, f32[4,128,128]{2,1,0:T(8,128)S(1)}, u32[]{:S(2)}, u32[]{:S(2)}) collective-permute-start(f32[4,128,128]{2,1,0:T(8,128)S(1)} %multiply_add_fusion.5), channel_id=1, source_target_pairs={{0,8},{8,16},{16,24},{24,32},{32,40},{40,48},{48,56},{56,64},{64,7... | collective-permute-start | bytes 786440 | tf_op jit(solution)/shard_map/ppermute | solution.py:17
  18.8 0.2 fusion.20
  19.0 2.4 %collective-permute-start.9 = (bf16[2,128,4,128]{3,1,2,0:T(8,128)(2,1)S(1)}, bf16[2,128,4,128]{3,1,2,0:T(8,128)(2,1)S(1)}, u32[]{:S(2)}, u32[]{:S(2)}) collective-permute-start(bf16[2,128,4,128]{3,1,2,0:T(8,128)(2,1)S(1)} %collective-permute-done.8), channel_id=1, source_target_pairs={{0,8},{8,16},{16,24},{24,32},{32,40},{40,48},{48,56},{56,64},{64,7... | collective-permute-start | bytes 786440 | tf_op jit(solution)/shard_map/ppermute | solution.py:17
  21.4 3.2 %collective-permute-done.1 = f32[4,128,128]{2,1,0:T(8,128)S(1)} collective-permute-done((f32[4,128,128]{2,1,0:T(8,128)S(1)}, f32[4,128,128]{2,1,0:T(8,128)S(1)}, u32[]{:S(2)}, u32[]{:S(2)}) %collective-permute-start.1) | collective-permute-done | bytes 262176 | tf_op jit(solution)/shard_map/ppermute | solution.py:17
  24.7 1.9 %collective-permute-start.2 = (f32[4,128,128]{2,1,0:T(8,128)S(1)}, f32[4,128,128]{2,1,0:T(8,128)S(1)}, u32[]{:S(2)}, u32[]{:S(2)}) collective-permute-start(f32[4,128,128]{2,1,0:T(8,128)S(1)} %multiply_add_fusion.4), channel_id=1, source_target_pairs={{0,8},{8,16},{16,24},{24,32},{32,40},{40,48},{48,56},{56,64},{64,7... | collective-permute-start | bytes 786440 | tf_op jit(solution)/shard_map/ppermute | solution.py:17
  27.0 0.2 convolution_bitcast_fusion.10
  27.2 0.3 collective-permute-done.9
  27.5 1.9 %collective-permute-start.10 = (bf16[2,128,4,128]{3,1,2,0:T(8,128)(2,1)S(1)}, bf16[2,128,4,128]{3,1,2,0:T(8,128)(2,1)S(1)}, u32[]{:S(2)}, u32[]{:S(2)}) collective-permute-start(bf16[2,128,4,128]{3,1,2,0:T(8,128)(2,1)S(1)} %collective-permute-done.9), channel_id=1, source_target_pairs={{0,8},{8,16},{16,24},{24,32},{32,40},{40,48},{48,56},{56,64},{64,7... | collective-permute-start | bytes 786440 | tf_op jit(solution)/shard_map/ppermute | solution.py:17
  29.4 5.1 %collective-permute-done.2 = f32[4,128,128]{2,1,0:T(8,128)S(1)} collective-permute-done((f32[4,128,128]{2,1,0:T(8,128)S(1)}, f32[4,128,128]{2,1,0:T(8,128)S(1)}, u32[]{:S(2)}, u32[]{:S(2)}) %collective-permute-start.2) | collective-permute-done | bytes 262176 | tf_op jit(solution)/shard_map/ppermute | solution.py:17
  34.6 1.9 %collective-permute-start.3 = (bf16[4,128,128]{2,1,0:T(8,128)(2,1)S(1)}, bf16[4,128,128]{2,1,0:T(8,128)(2,1)S(1)}, u32[]{:S(2)}, u32[]{:S(2)}) collective-permute-start(bf16[4,128,128]{2,1,0:T(8,128)(2,1)S(1)} %multiply_add_fusion.3), channel_id=1, source_target_pairs={{0,8},{8,16},{16,24},{24,32},{32,40},{40,48},{48,56},{56,64},{64,7... | collective-permute-start | bytes 393224 | tf_op jit(solution)/shard_map/ppermute | solution.py:17
  36.7 0.6 collective-permute-done.10
  37.3 1.9 %collective-permute-start.11 = (bf16[2,128,4,128]{3,1,2,0:T(8,128)(2,1)S(1)}, bf16[2,128,4,128]{3,1,2,0:T(8,128)(2,1)S(1)}, u32[]{:S(2)}, u32[]{:S(2)}) collective-permute-start(bf16[2,128,4,128]{3,1,2,0:T(8,128)(2,1)S(1)} %collective-permute-done.10), channel_id=1, source_target_pairs={{0,8},{8,16},{16,24},{24,32},{32,40},{40,48},{48,56},{56,64},{64,7... | collective-permute-start | bytes 786440 | tf_op jit(solution)/shard_map/ppermute | solution.py:17
  39.2 5.1 %collective-permute-done.3 = bf16[4,128,128]{2,1,0:T(8,128)(2,1)S(1)} collective-permute-done((bf16[4,128,128]{2,1,0:T(8,128)(2,1)S(1)}, bf16[4,128,128]{2,1,0:T(8,128)(2,1)S(1)}, u32[]{:S(2)}, u32[]{:S(2)}) %collective-permute-start.3) | collective-permute-done | bytes 131104 | tf_op jit(solution)/shard_map/ppermute | solution.py:17
  44.3 0.3 multiply_reduce_fusion.1
  44.5 13.9 %all-reduce = (f32[128]{0:T(128)S(1)}, f32[128]{0:T(128)S(1)}) all-reduce(f32[128]{0:T(128)S(1)} %get-tuple-element.25, f32[128]{0:T(128)S(1)} %get-tuple-element.24), channel_id=1, replica_groups=mesh['ctx'=64,'head'=8] {'head'}, use_global_device_ids=true, to_apply=%region_2.3 | all-reduce | flops 256 | bytes 2048 | tf_op jit(solution)/shard_map/psum | solution.py:69
  58.4 0.8 subtract_convert_fusion
  59.4 0.4 fusion.56
  59.8 0.2 fusion.14
  60.0 1.2 multiply_reduce_fusion
  61.2 0.3 convolution_bitcast_fusion
  61.5 0.4 fusion.4
  62.0 0.3 convolution_bitcast_fusion.1
  62.4 0.5 copy-done.4
  62.8 11.3 %collective-permute-start.12 = (f32[2,128,4,128]{3,1,2,0:T(8,128)S(1)}, f32[2,128,4,128]{3,1,2,0:T(8,128)S(1)}, u32[]{:S(2)}, u32[]{:S(2)}) collective-permute-start(f32[2,128,4,128]{3,1,2,0:T(8,128)S(1)} %fusion.30), channel_id=1, source_target_pairs={{8,0},{16,8},{24,16},{32,24},{40,32},{48,40},{56,48},{64,56},{72,6... | collective-permute-start | bytes 1572872 | tf_op jit(solution)/shard_map/ppermute | solution.py:17
  74.1 0.2 broadcast_add_fusion
  74.4 1.9 %collective-permute-start.4 = (f32[4,128,128]{2,1,0:T(8,128)S(1)}, f32[4,128,128]{2,1,0:T(8,128)S(1)}, u32[]{:S(2)}, u32[]{:S(2)}) collective-permute-start(f32[4,128,128]{2,1,0:T(8,128)S(1)} %get-tuple-element.41), channel_id=1, source_target_pairs={{8,0},{16,8},{24,16},{32,24},{40,32},{48,40},{56,48},{64,56},{72,6... | collective-permute-start | bytes 786440 | tf_op jit(solution)/shard_map/ppermute | solution.py:17
  76.3 0.2 fusion.21
  76.6 5.5 %collective-permute-done.4 = f32[4,128,128]{2,1,0:T(8,128)S(1)} collective-permute-done((f32[4,128,128]{2,1,0:T(8,128)S(1)}, f32[4,128,128]{2,1,0:T(8,128)S(1)}, u32[]{:S(2)}, u32[]{:S(2)}) %collective-permute-start.4) | collective-permute-done | bytes 262176 | tf_op jit(solution)/shard_map/ppermute | solution.py:17
  82.2 3.6 %collective-permute-start.5 = (f32[4,128,128]{2,1,0:T(8,128)S(1)}, f32[4,128,128]{2,1,0:T(8,128)S(1)}, u32[]{:S(2)}, u32[]{:S(2)}) collective-permute-start(f32[4,128,128]{2,1,0:T(8,128)S(1)} %multiply_add_fusion.2), channel_id=1, source_target_pairs={{8,0},{16,8},{24,16},{32,24},{40,32},{48,40},{56,48},{64,56},{72,6... | collective-permute-start | bytes 786440 | tf_op jit(solution)/shard_map/ppermute | solution.py:17
  85.9 5.9 %collective-permute-start.13 = (f32[2,128,4,128]{3,1,2,0:T(8,128)S(1)}, f32[2,128,4,128]{3,1,2,0:T(8,128)S(1)}, u32[]{:S(2)}, u32[]{:S(2)}) collective-permute-start(f32[2,128,4,128]{3,1,2,0:T(8,128)S(1)} %fusion.32), channel_id=1, source_target_pairs={{8,0},{16,8},{24,16},{32,24},{40,32},{48,40},{56,48},{64,56},{72,6... | collective-permute-start | bytes 1572872 | tf_op jit(solution)/shard_map/ppermute | solution.py:17
  91.8 0.2 convolution_bitcast_fusion.8
  92.1 0.8 fusion.17
  92.9 0.8 multiply_add_fusion.1
  93.7 2.8 %collective-permute-start.6 = (f32[4,128,128]{2,1,0:T(8,128)}, f32[4,128,128]{2,1,0:T(8,128)}, u32[]{:S(2)}, u32[]{:S(2)}) collective-permute-start(f32[4,128,128]{2,1,0:T(8,128)} %multiply_add_fusion.1), channel_id=1, source_target_pairs={{8,0},{16,8},{24,16},{32,24},{40,32},{48,40},{56,48},{64,56},{72,6... | collective-permute-start | bytes 786440 | tf_op jit(solution)/shard_map/ppermute | solution.py:17
  96.5 0.9 fusion.34
  97.4 5.9 %collective-permute-start.14 = (f32[2,128,4,128]{3,1,2,0:T(8,128)}, f32[2,128,4,128]{3,1,2,0:T(8,128)}, u32[]{:S(2)}, u32[]{:S(2)}) collective-permute-start(f32[2,128,4,128]{3,1,2,0:T(8,128)} %fusion.34), channel_id=1, source_target_pairs={{8,0},{16,8},{24,16},{32,24},{40,32},{48,40},{56,48},{64,56},{72,6... | collective-permute-start | bytes 1572872 | tf_op jit(solution)/shard_map/ppermute | solution.py:17
  103.4 0.9 convolution_bitcast_fusion.4
  104.3 1.7 %copy.97 = bf16[128,4,128]{2,1,0:T(4,128)(2,1)} copy(bf16[128,4,128]{0,2,1:T(8,128)(2,1)} %get-tuple-element.29) | data formatting | bytes 262144
  106.0 1.7 %copy.98 = bf16[128,4,128]{2,1,0:T(4,128)(2,1)} copy(bf16[128,4,128]{0,2,1:T(8,128)(2,1)} %fusion.17) | data formatting | bytes 262144
  107.7 1.8 %convolution_bitcast_fusion.6 = f32[128,4,128]{2,0,1:T(8,128)} fusion(bf16[4,128,128]{2,1,0:T(8,128)(2,1)} %copy-done.10, bf16[128,4,128]{0,2,1:T(8,128)(2,1)S(1)} %copy.78), kind=kOutput, calls=%fused_computation.29 | convolution fusion | flops 16777216 | bytes 524288 | tf_op jit(solution)/shard_map/hts,thd->shd/dot_general | solution.py:92
  109.5 1.7 %multiply_add_fusion = bf16[4,128,128]{2,1,0:T(8,128)(2,1)} fusion(f32[4,128,128]{2,1,0:T(8,128)S(1)} %get-tuple-element.42, f32[4,128,128]{2,1,0:T(8,128)} %collective-permute-done.6, f32[4]{0:T(128)S(1)} %slice_reduce_fusion.1), kind=kLoop, calls=%fused_computation.67 | loop fusion | flops 196608 | bytes 655376 | tf_op jit(solution)/shard_map/add | solution.py:82
  111.2 4.8 %collective-permute-start.7 = (bf16[4,128,128]{2,1,0:T(8,128)(2,1)}, bf16[4,128,128]{2,1,0:T(8,128)(2,1)S(1)}, u32[]{:S(2)}, u32[]{:S(2)}) collective-permute-start(bf16[4,128,128]{2,1,0:T(8,128)(2,1)} %multiply_add_fusion), channel_id=1, source_target_pairs={{8,0},{16,8},{24,16},{32,24},{40,32},{48,40},{56,48},{64,56},{72,6... | collective-permute-start | bytes 393224 | tf_op jit(solution)/shard_map/ppermute | solution.py:17
  116.0 1.9 %fusion.29 = f32[2,128,4,128]{3,1,2,0:T(8,128)} fusion(f32[2,128,4,128]{3,1,2,0:T(8,128)} %collective-permute-done.14, f32[1,640,4,128]{3,1,2,0:T(8,128)S(1)} %convolution_bitcast_fusion.1, f32[1,640,4,128]{3,1,2,0:T(8,128)S(1)} %convolution_bitcast_fusion), kind=kLoop, calls=%fused_computation.55 | loop fusion | flops 262144 | bytes 3670016 | tf_op jit(solution)/shard_map/add | solution.py:153
  117.9 2.0 %collective-permute-start.15 = (f32[2,128,4,128]{3,1,2,0:T(8,128)}, f32[2,128,4,128]{3,1,2,0:T(8,128)}, u32[]{:S(2)}, u32[]{:S(2)}) collective-permute-start(f32[2,128,4,128]{3,1,2,0:T(8,128)} %fusion.29), channel_id=1, source_target_pairs={{8,0},{16,8},{24,16},{32,24},{40,32},{48,40},{56,48},{64,56},{72,6... | collective-permute-start | bytes 1572872 | tf_op jit(solution)/shard_map/ppermute | solution.py:17
  120.0 1.1 fusion.23
  121.1 0.8 copy.101
  121.9 1.7 %copy.102 = bf16[128,4,128]{2,1,0:T(4,128)(2,1)} copy(bf16[128,4,128]{0,2,1:T(8,128)(2,1)} %fusion.23) | data formatting | bytes 262144
  123.6 1.2 fusion.18
  124.7 0.8 copy.99
  125.5 0.2 fusion.19
  125.7 0.8 copy.100
  126.4 2.5 %collective-permute-done.15 = f32[2,128,4,128]{3,1,2,0:T(8,128)} collective-permute-done((f32[2,128,4,128]{3,1,2,0:T(8,128)}, f32[2,128,4,128]{3,1,2,0:T(8,128)}, u32[]{:S(2)}, u32[]{:S(2)}) %collective-permute-start.15) | collective-permute-done | bytes 524320 | tf_op jit(solution)/shard_map/ppermute | solution.py:17
  128.9 1.1 fusion.36
  130.0 0.8 copy.104
  130.8 0.8 copy.103
  (78 shorter events, 1.7 us)
Async XLA Ops:
  0.6 58.8 %copy-start = (bf16[128,4,128]{2,1,0:T(4,128)(2,1)S(1)}, bf16[128,4,128]{2,1,0:T(4,128)(2,1)}, u32[]{:S(2)}) copy-start(bf16[128,4,128]{2,1,0:T(4,128)(2,1)} %param.17) | copy-start | bytes 393220
  0.6 13.1 %copy-start.20 = (s32[128]{0:T(128)S(1)}, s32[128]{0:T(128)}, u32[]{:S(2)}) copy-start(s32[128]{0:T(128)} %param.21) | copy-start | bytes 1540
  4.7 9.3 %copy-start.21 = (f32[4]{0:T(128)}, f32[4]{0:T(128)S(1)}, u32[]{:S(2)}) copy-start(f32[4]{0:T(128)S(1)} %broadcast_multiply_fusion.1) | copy-start | bytes 52
  4.7 13.9 %copy-start.11 = (bf16[128,4,128]{2,1,0:T(4,128)(2,1)S(1)}, bf16[128,4,128]{2,1,0:T(4,128)(2,1)}, u32[]{:S(2)}) copy-start(bf16[128,4,128]{2,1,0:T(4,128)(2,1)} %param.11) | copy-start | bytes 393220
  4.7 14.0 %copy-start.2 = (bf16[128,4,128]{2,1,0:T(4,128)(2,1)S(1)}, bf16[128,4,128]{2,1,0:T(4,128)(2,1)}, u32[]{:S(2)}) copy-start(bf16[128,4,128]{2,1,0:T(4,128)(2,1)} %param.12) | copy-start | bytes 393220
  6.1 7.9 %collective-permute-start = (f32[4,128,128]{2,1,0:T(8,128)S(1)}, f32[4,128,128]{2,1,0:T(8,128)S(1)}, u32[]{:S(2)}, u32[]{:S(2)}) collective-permute-start(f32[4,128,128]{2,1,0:T(8,128)S(1)} %get-tuple-element.38), channel_id=1, source_target_pairs={{0,8},{8,16},{16,24},{24,32},{32,40},{40,48},{48,56},{56,64},{64,7... | collective-permute-start | bytes 786440 | tf_op jit(solution)/shard_map/ppermute | solution.py:17
  11.7 15.0 %copy-start.12 = (bf16[128,4,128]{2,1,0:T(4,128)(2,1)S(1)}, bf16[128,4,128]{2,1,0:T(4,128)(2,1)}, u32[]{:S(2)}) copy-start(bf16[128,4,128]{2,1,0:T(4,128)(2,1)} %param.20) | copy-start | bytes 393220
  11.7 7.3 %collective-permute-start.8 = (bf16[2,128,4,128]{3,1,2,0:T(8,128)(2,1)S(1)}, bf16[2,128,4,128]{3,1,2,0:T(8,128)(2,1)S(1)}, u32[]{:S(2)}, u32[]{:S(2)}) collective-permute-start(bf16[2,128,4,128]{3,1,2,0:T(8,128)(2,1)S(1)} %pad_maximum_fusion.1), channel_id=1, source_target_pairs={{0,8},{8,16},{16,24},{24,32},{32,40},{40,48},{48,56},{56,64},{64,7... | collective-permute-start | bytes 786440 | tf_op jit(solution)/shard_map/ppermute | solution.py:17
  13.9 13.0 %copy-start.17 = (pred[128,128]{1,0:T(8,128)(4,1)}, pred[128,128]{1,0:T(8,128)(4,1)S(1)}, u32[]{:S(2)}) copy-start(pred[128,128]{1,0:T(8,128)(4,1)S(1)} %fusion.55) | copy-start | bytes 49156
  13.9 12.9 %copy-start.13 = (bf16[128,4,128]{2,1,0:T(4,128)(2,1)S(1)}, bf16[128,4,128]{2,1,0:T(4,128)(2,1)}, u32[]{:S(2)}) copy-start(bf16[128,4,128]{2,1,0:T(4,128)(2,1)} %param.16) | copy-start | bytes 393220
  14.0 12.9 %copy-start.1 = (bf16[128,4,128]{2,1,0:T(4,128)(2,1)S(1)}, bf16[128,4,128]{2,1,0:T(4,128)(2,1)}, u32[]{:S(2)}) copy-start(bf16[128,4,128]{2,1,0:T(4,128)(2,1)} %param.13) | copy-start | bytes 393220
  14.1 10.6 %collective-permute-start.1 = (f32[4,128,128]{2,1,0:T(8,128)S(1)}, f32[4,128,128]{2,1,0:T(8,128)S(1)}, u32[]{:S(2)}, u32[]{:S(2)}) collective-permute-start(f32[4,128,128]{2,1,0:T(8,128)S(1)} %multiply_add_fusion.5), channel_id=1, source_target_pairs={{0,8},{8,16},{16,24},{24,32},{32,40},{40,48},{48,56},{56,64},{64,7... | collective-permute-start | bytes 786440 | tf_op jit(solution)/shard_map/ppermute | solution.py:17
  19.0 25.2 %copy-start.8 = (bf16[4,128,128]{2,1,0:T(8,128)(2,1)}, bf16[4,128,128]{2,1,0:T(8,128)(2,1)S(1)}, u32[]{:S(2)}) copy-start(bf16[4,128,128]{2,1,0:T(8,128)(2,1)S(1)} %fusion.20) | copy-start | bytes 393220
  19.0 25.2 %copy-start.19 = (f32[4,128]{1,0:T(4,128)S(1)}, f32[4,128]{1,0:T(4,128)}, u32[]{:S(2)}) copy-start(f32[4,128]{1,0:T(4,128)} %param.15) | copy-start | bytes 6148
  19.0 8.4 %collective-permute-start.9 = (bf16[2,128,4,128]{3,1,2,0:T(8,128)(2,1)S(1)}, bf16[2,128,4,128]{3,1,2,0:T(8,128)(2,1)S(1)}, u32[]{:S(2)}, u32[]{:S(2)}) collective-permute-start(bf16[2,128,4,128]{3,1,2,0:T(8,128)(2,1)S(1)} %collective-permute-done.8), channel_id=1, source_target_pairs={{0,8},{8,16},{16,24},{24,32},{32,40},{40,48},{48,56},{56,64},{64,7... | collective-permute-start | bytes 786440 | tf_op jit(solution)/shard_map/ppermute | solution.py:17
  24.7 9.8 %collective-permute-start.2 = (f32[4,128,128]{2,1,0:T(8,128)S(1)}, f32[4,128,128]{2,1,0:T(8,128)S(1)}, u32[]{:S(2)}, u32[]{:S(2)}) collective-permute-start(f32[4,128,128]{2,1,0:T(8,128)S(1)} %multiply_add_fusion.4), channel_id=1, source_target_pairs={{0,8},{8,16},{16,24},{24,32},{32,40},{40,48},{48,56},{56,64},{64,7... | collective-permute-start | bytes 786440 | tf_op jit(solution)/shard_map/ppermute | solution.py:17
  27.5 9.8 %collective-permute-start.10 = (bf16[2,128,4,128]{3,1,2,0:T(8,128)(2,1)S(1)}, bf16[2,128,4,128]{3,1,2,0:T(8,128)(2,1)S(1)}, u32[]{:S(2)}, u32[]{:S(2)}) collective-permute-start(bf16[2,128,4,128]{3,1,2,0:T(8,128)(2,1)S(1)} %collective-permute-done.9), channel_id=1, source_target_pairs={{0,8},{8,16},{16,24},{24,32},{32,40},{40,48},{48,56},{56,64},{64,7... | collective-permute-start | bytes 786440 | tf_op jit(solution)/shard_map/ppermute | solution.py:17
  34.6 9.6 %collective-permute-start.3 = (bf16[4,128,128]{2,1,0:T(8,128)(2,1)S(1)}, bf16[4,128,128]{2,1,0:T(8,128)(2,1)S(1)}, u32[]{:S(2)}, u32[]{:S(2)}) collective-permute-start(bf16[4,128,128]{2,1,0:T(8,128)(2,1)S(1)} %multiply_add_fusion.3), channel_id=1, source_target_pairs={{0,8},{8,16},{16,24},{24,32},{32,40},{40,48},{48,56},{56,64},{64,7... | collective-permute-start | bytes 393224 | tf_op jit(solution)/shard_map/ppermute | solution.py:17
  37.3 21.9 %collective-permute-start.11 = (bf16[2,128,4,128]{3,1,2,0:T(8,128)(2,1)S(1)}, bf16[2,128,4,128]{3,1,2,0:T(8,128)(2,1)S(1)}, u32[]{:S(2)}, u32[]{:S(2)}) collective-permute-start(bf16[2,128,4,128]{3,1,2,0:T(8,128)(2,1)S(1)} %collective-permute-done.10), channel_id=1, source_target_pairs={{0,8},{8,16},{16,24},{24,32},{32,40},{40,48},{48,56},{56,64},{64,7... | collective-permute-start | bytes 786440 | tf_op jit(solution)/shard_map/ppermute | solution.py:17
  44.2 15.0 %copy-start.6 = (bf16[4,128,128]{2,1,0:T(8,128)(2,1)}, bf16[4,128,128]{2,1,0:T(8,128)(2,1)S(1)}, u32[]{:S(2)}) copy-start(bf16[4,128,128]{2,1,0:T(8,128)(2,1)S(1)} %collective-permute-done.3) | copy-start | bytes 393220
  59.4 2.1 %copy-start.15 = (bf16[2,640,4,128]{3,1,2,0:T(8,128)(2,1)}, bf16[2,640,4,128]{3,1,2,0:T(8,128)(2,1)S(1)}, u32[]{:S(2)}) copy-start(bf16[2,640,4,128]{3,1,2,0:T(8,128)(2,1)S(1)} %constant_dynamic-update-slice_fusion) | copy-start | bytes 3932164
  62.0 0.9 copy-start.4
  62.3 11.8 %copy-start.22 = (f32[4]{0:T(128)S(1)}, f32[4]{0:T(128)}, u32[]{:S(2)}) copy-start(f32[4]{0:T(128)} %copy-done.21) | copy-start | bytes 52
  62.3 14.0 %copy-start.18 = (pred[128,128]{1,0:T(8,128)(4,1)S(1)}, pred[128,128]{1,0:T(8,128)(4,1)}, u32[]{:S(2)}) copy-start(pred[128,128]{1,0:T(8,128)(4,1)} %copy-done.17) | copy-start | bytes 49156
  62.8 23.0 %collective-permute-start.12 = (f32[2,128,4,128]{3,1,2,0:T(8,128)S(1)}, f32[2,128,4,128]{3,1,2,0:T(8,128)S(1)}, u32[]{:S(2)}, u32[]{:S(2)}) collective-permute-start(f32[2,128,4,128]{3,1,2,0:T(8,128)S(1)} %fusion.30), channel_id=1, source_target_pairs={{8,0},{16,8},{24,16},{32,24},{40,32},{48,40},{56,48},{64,56},{72,6... | collective-permute-start | bytes 1572872 | tf_op jit(solution)/shard_map/ppermute | solution.py:17
  74.4 7.7 %collective-permute-start.4 = (f32[4,128,128]{2,1,0:T(8,128)S(1)}, f32[4,128,128]{2,1,0:T(8,128)S(1)}, u32[]{:S(2)}, u32[]{:S(2)}) collective-permute-start(f32[4,128,128]{2,1,0:T(8,128)S(1)} %get-tuple-element.41), channel_id=1, source_target_pairs={{8,0},{16,8},{24,16},{32,24},{40,32},{48,40},{56,48},{64,56},{72,6... | collective-permute-start | bytes 786440 | tf_op jit(solution)/shard_map/ppermute | solution.py:17
  76.5 15.3 %copy-start.10 = (bf16[4,128,128]{2,1,0:T(8,128)(2,1)}, bf16[4,128,128]{2,1,0:T(8,128)(2,1)S(1)}, u32[]{:S(2)}) copy-start(bf16[4,128,128]{2,1,0:T(8,128)(2,1)S(1)} %fusion.21) | copy-start | bytes 393220
  82.1 9.9 %copy-start.7 = (bf16[4,128,128]{2,1,0:T(8,128)(2,1)S(1)}, bf16[4,128,128]{2,1,0:T(8,128)(2,1)}, u32[]{:S(2)}) copy-start(bf16[4,128,128]{2,1,0:T(8,128)(2,1)} %copy-done.6) | copy-start | bytes 393220
  82.2 10.8 %collective-permute-start.5 = (f32[4,128,128]{2,1,0:T(8,128)S(1)}, f32[4,128,128]{2,1,0:T(8,128)S(1)}, u32[]{:S(2)}, u32[]{:S(2)}) collective-permute-start(f32[4,128,128]{2,1,0:T(8,128)S(1)} %multiply_add_fusion.2), channel_id=1, source_target_pairs={{8,0},{16,8},{24,16},{32,24},{40,32},{48,40},{56,48},{64,56},{72,6... | collective-permute-start | bytes 786440 | tf_op jit(solution)/shard_map/ppermute | solution.py:17
  85.9 10.6 %collective-permute-start.13 = (f32[2,128,4,128]{3,1,2,0:T(8,128)S(1)}, f32[2,128,4,128]{3,1,2,0:T(8,128)S(1)}, u32[]{:S(2)}, u32[]{:S(2)}) collective-permute-start(f32[2,128,4,128]{3,1,2,0:T(8,128)S(1)} %fusion.32), channel_id=1, source_target_pairs={{8,0},{16,8},{24,16},{32,24},{40,32},{48,40},{56,48},{64,56},{72,6... | collective-permute-start | bytes 1572872 | tf_op jit(solution)/shard_map/ppermute | solution.py:17
  93.7 9.6 %copy-start.9 = (bf16[4,128,128]{2,1,0:T(8,128)(2,1)S(1)}, bf16[4,128,128]{2,1,0:T(8,128)(2,1)}, u32[]{:S(2)}) copy-start(bf16[4,128,128]{2,1,0:T(8,128)(2,1)} %copy-done.8) | copy-start | bytes 393220
  93.7 15.8 %collective-permute-start.6 = (f32[4,128,128]{2,1,0:T(8,128)}, f32[4,128,128]{2,1,0:T(8,128)}, u32[]{:S(2)}, u32[]{:S(2)}) collective-permute-start(f32[4,128,128]{2,1,0:T(8,128)} %multiply_add_fusion.1), channel_id=1, source_target_pairs={{8,0},{16,8},{24,16},{32,24},{40,32},{48,40},{56,48},{64,56},{72,6... | collective-permute-start | bytes 786440 | tf_op jit(solution)/shard_map/ppermute | solution.py:17
  97.4 18.6 %collective-permute-start.14 = (f32[2,128,4,128]{3,1,2,0:T(8,128)}, f32[2,128,4,128]{3,1,2,0:T(8,128)}, u32[]{:S(2)}, u32[]{:S(2)}) collective-permute-start(f32[2,128,4,128]{3,1,2,0:T(8,128)} %fusion.34), channel_id=1, source_target_pairs={{8,0},{16,8},{24,16},{32,24},{40,32},{48,40},{56,48},{64,56},{72,6... | collective-permute-start | bytes 1572872 | tf_op jit(solution)/shard_map/ppermute | solution.py:17
  111.2 8.8 %copy-start.5 = (bf16[4,128,640]{1,2,0:T(8,128)(2,1)S(1)}, bf16[4,128,640]{1,2,0:T(8,128)(2,1)}, u32[]{:S(2)}) copy-start(bf16[4,128,640]{1,2,0:T(8,128)(2,1)} %copy-done.4) | copy-start | bytes 1966084
  111.2 8.8 %copy-start.16 = (bf16[2,640,4,128]{3,1,2,0:T(8,128)(2,1)S(1)}, bf16[2,640,4,128]{3,1,2,0:T(8,128)(2,1)}, u32[]{:S(2)}) copy-start(bf16[2,640,4,128]{3,1,2,0:T(8,128)(2,1)} %copy-done.15) | copy-start | bytes 3932164
  111.2 12.3 %collective-permute-start.7 = (bf16[4,128,128]{2,1,0:T(8,128)(2,1)}, bf16[4,128,128]{2,1,0:T(8,128)(2,1)S(1)}, u32[]{:S(2)}, u32[]{:S(2)}) collective-permute-start(bf16[4,128,128]{2,1,0:T(8,128)(2,1)} %multiply_add_fusion), channel_id=1, source_target_pairs={{8,0},{16,8},{24,16},{32,24},{40,32},{48,40},{56,48},{64,56},{72,6... | collective-permute-start | bytes 393224 | tf_op jit(solution)/shard_map/ppermute | solution.py:17
  117.9 3.1 %copy-start.14 = (bf16[128,4,128]{0,2,1:T(8,128)(2,1)S(1)}, bf16[128,4,128]{0,2,1:T(8,128)(2,1)}, u32[]{:S(2)}) copy-start(bf16[128,4,128]{0,2,1:T(8,128)(2,1)} %get-tuple-element.46) | copy-start | bytes 393220
  117.9 7.5 %copy-start.3 = (f32[128,4,128]{2,0,1:T(8,128)S(1)}, f32[128,4,128]{2,0,1:T(8,128)}, u32[]{:S(2)}) copy-start(f32[128,4,128]{2,0,1:T(8,128)} %convolution_bitcast_fusion.4) | copy-start | bytes 786436
  117.9 10.9 %collective-permute-start.15 = (f32[2,128,4,128]{3,1,2,0:T(8,128)}, f32[2,128,4,128]{3,1,2,0:T(8,128)}, u32[]{:S(2)}, u32[]{:S(2)}) collective-permute-start(f32[2,128,4,128]{3,1,2,0:T(8,128)} %fusion.29), channel_id=1, source_target_pairs={{8,0},{16,8},{24,16},{32,24},{40,32},{48,40},{56,48},{64,56},{72,6... | collective-permute-start | bytes 1572872 | tf_op jit(solution)/shard_map/ppermute | solution.py:17
where the time goes:
time: 132 us
  starting transfers between devices  59.5 us (45%)
  waiting for transfers between devices  22.2 us (17%)
  blocking collectives  13.9 us (11%)
  local copies, waits for them, and re-layouts  12.7 us (10%)
  matrix products  11.4 us (9%)
  other arithmetic  10.6 us (8%)
    ppermute x16, starting transfers between devices, from_behind(): lax.ppermute(value, axis, [(source, source + steps) for source in range(i...  59.5 us
    ppermute x16, waiting for transfers between devices, from_behind(): lax.ppermute(value, axis, [(source, source + steps) for source in range(i...  22.2 us
    psum x1, blocking collectives, shards(): lax.psum((jnp.sum(raw_out * raw_out, axis=(1, 2)), jnp.sum(gained * raw_o...  13.9 us
    unnamed x61, local copies, waits for them, and re-layouts  10 us
    add x3, other arithmetic, shards(): from_behind(returning, 'ctx', -1)  2.91 us
  transfers between devices with their start and end apart: 16, of which 8 were waited for; matrix products, arithmetic and copies ran while one was open for 18% of the time, Pallas kernels for 0%

commit v1 on v0

v1 whole, which is shorter than its diff:
```python
import functools
import math

import jax
import jax.numpy as jnp
from jax import lax
from jax.experimental import pallas as pl
from jax.experimental.pallas import tpu as pltpu
from jax.sharding import PartitionSpec as P

SPAN = 4
NORM_EPS = 1e-05
MASKED = -1e30
MESH = pl.DeviceIdType.MESH
F32 = jnp.float32
BF16 = jnp.bfloat16

LQ, LK, LV, LC, SQ, SK, SV, SC = range(8)
O_LIN, O_LQ, O_LK, O_LV, O_SOFT, O_SQ, O_SK, O_SV = range(8)


def dot_nn(a, b):
    return lax.dot_general(a, b, (((1,), (0,)), ((), ())), preferred_element_type=F32)


def dot_nt(a, b):
    return lax.dot_general(a, b, (((1,), (1,)), ((), ())), preferred_element_type=F32)


def dot_tn(a, b):
    return lax.dot_general(a, b, (((0,), (0,)), ((), ())), preferred_element_type=F32)


def kernel(n_ctx, n_head, heads, tok, size, *refs):
    ins = refs[:8]
    ld_in, ng_in, ds_in = refs[8:11]
    outs = refs[11:19]
    (
        raw, stage, hb, kv, ldv, ngv, dsv, bias, mask, enter, leave, within,
        gacc, gsend, grecv, fsend, frecv, nsend, nrecv,
        cl, clr, ptile, comb, x0b, ssend, srecv, tsend, trecv, isend, st,
        ysend, yrecv, attend, rawo, rgrad, pu, pur, rsend, rrecv, qsend, qrecv, osend, back,
        dkp, dvp, ostage, obf,
        in_sem, out_sem, small_sem, fwd_s, fwd_r, bwd_s, bwd_r, lin_s, lin_r, y_s, y_r,
    ) = refs[19:]
    half = heads // 2
    span = SPAN * tok
    width = span + tok
    me = lax.axis_index("ctx")
    hd = lax.axis_index("head")
    k = lax.rem(me, 2)
    first = k == 0
    par = me + 1 - 2 * k
    nxt = lax.rem(me + 2, n_ctx)
    prv = lax.rem(me + n_ctx - 2, n_ctx)
    inv_root = 1.0 / math.sqrt(size)

    def rows(slot):
        return pl.ds(pl.multiple_of(slot * tok, tok), tok)

    window = pl.ds(pl.multiple_of(k * tok, tok), width)

    def remote(src, dst, send, recv, where):
        return pltpu.make_async_remote_copy(
            src_ref=src, dst_ref=dst, send_sem=send, recv_sem=recv,
            device_id=(where, hd), device_id_type=MESH,
        )

    barrier = pltpu.get_barrier_semaphore()
    for other in (par, nxt, prv):
        pl.semaphore_signal(barrier, inc=1, device_id=(other, hd), device_id_type=MESH)
    for step in range(1, n_head):
        pl.semaphore_signal(
            barrier, inc=1, device_id=(me, lax.rem(hd + step, n_head)), device_id_type=MESH
        )

    loads = {}
    for i in (SK, SV, LK, LV, LQ, SQ, SC, LC):
        loads[i] = pltpu.make_async_copy(ins[i], raw.at[i], in_sem.at[i])
    small = [
        pltpu.make_async_copy(ds_in, dsv, small_sem.at[0]),
        pltpu.make_async_copy(ld_in, ldv, small_sem.at[1]),
        pltpu.make_async_copy(ng_in, ngv, small_sem.at[2]),
    ]
    for i in (SK, SV):
        loads[i].start()
    for copy in small:
        copy.start()
    for i in (LK, LV, LQ, SQ, SC, LC):
        loads[i].start()

    def head_of(i, h):
        return stage[i, pl.ds(h, tok, stride=heads), :]

    def unpack(i):
        loads[i].wait()
        stage[i] = raw[i].astype(F32)

    for i, part in ((SK, 0), (SV, 1)):
        unpack(i)
        for h in range(heads):
            kv[h, part, rows(4 + k), :] = head_of(i, h).astype(BF16)
    pl.semaphore_wait(barrier, 2 + n_head)

    def fwd_copy(kind, h):
        if kind == 0:
            src, dst, where = 4 + k, 2 + k, nxt
        elif kind == 1:
            src, dst, where = 2 + k, k, nxt
        elif kind == 2:
            src, dst, where = 4 - k, 4 - k, par
        else:
            src, dst, where = 2 - k, 2 - k, par
        return remote(
            kv.at[h, :, rows(src), :], kv.at[h, :, rows(dst), :],
            fwd_s.at[kind, h], fwd_r.at[kind, h], where,
        )

    fwd = {(kind, h): fwd_copy(kind, h) for kind in range(4) for h in range(heads)}

    def step_a(h):
        fwd[0, h].start()

    def step_b(h):
        fwd[0, h].wait_recv()
        fwd[1, h].start()
        fwd[2, h].start()

    def step_c(h):
        fwd[1, h].wait_recv()
        fwd[3, h].start()

    def step_d(h):
        fwd[2, h].wait_recv()
        fwd[3, h].wait_recv()

    step_a(0)
    step_a(1)

    for copy in small:
        copy.wait()
    t_pos = lax.broadcasted_iota(jnp.int32, (tok, tok), 0)
    s_pos = lax.broadcasted_iota(jnp.int32, (tok, tok), 1)
    first_row = (me * tok).astype(F32)
    ds_row = jnp.broadcast_to(dsv[...].astype(F32), (tok, tok))
    ds_col = jnp.transpose(ds_row)
    mask[...] = jnp.where((ds_row == ds_col) & (s_pos <= t_pos), 1.0, 0.0)
    ds_last = jnp.broadcast_to(ds_row[:, tok - 1 :], (tok, tok))
    triangle = jnp.where(t_pos <= s_pos, 1.0, 0.0).astype(F32)
    decays = jnp.concatenate([ldv[...], jnp.zeros((8 - heads, tok), F32)], axis=0)
    cumulative = lax.dot_general(
        decays, triangle, (((1,), (0,)), ((), ())),
        precision=lax.Precision.HIGHEST, preferred_element_type=F32,
    )
    for h in range(heads):
        cum_row = jnp.broadcast_to(cumulative[h : h + 1, :], (tok, tok))
        cum_col = jnp.transpose(cum_row)
        within[h] = jnp.where(mask[...] > 0.0, jnp.exp(jnp.minimum(cum_col - cum_row, 0.0)), 0.0)
        enter[h] = jnp.where(ds_col < first_row, jnp.exp(cum_col), 0.0)
        cum_last = jnp.broadcast_to(cum_row[:, tok - 1 :], (tok, tok))
        leave[h] = jnp.where(ds_col == ds_last, jnp.exp(cum_last - cum_col), 0.0)
        ptile[0, h : h + 1, :] = enter[h, tok - 1 :, :]
    ptile[0, heads:, :] = jnp.zeros((8 - heads, size), F32)

    for i, place in ((LK, 1), (LV, 2)):
        unpack(i)
        for h in range(heads):
            hb[place, h] = head_of(i, h).astype(BF16)

    for h in range(heads):
        keyed = (leave[h] * head_of(LK, h)).astype(BF16)
        cl[h] = dot_tn(keyed, hb[2, h])
    mine = pl.ds(2 * k, half)
    theirs = pl.ds(2 * (1 - k), half)
    cl_copy = remote(cl.at[theirs], clr, lin_s.at[0], lin_r.at[0], par)
    p_copy = remote(ptile.at[0], ptile.at[1], lin_s.at[1], lin_r.at[1], par)
    cl_copy.start()
    p_copy.start()

    for i, place in ((LQ, 0), (SQ, 3), (SC, 4)):
        unpack(i)
        for h in range(heads):
            hb[place, h] = head_of(i, h).astype(BF16)
    unpack(LC)
    for h in range(heads):
        scores = dot_nt(hb[0, h], hb[1, h])
        attend[h] = (within[h] * scores).astype(BF16)
        rawo[h] = dot_nn(attend[h], hb[2, h])

    q_index = lax.broadcasted_iota(jnp.int32, (tok, width), 0) + span
    k_index = lax.broadcasted_iota(jnp.int32, (tok, width), 1)
    ds_wide = jnp.broadcast_to(ds_col[:, :1], (tok, width)) - first_row + float(span)
    allowed = (k_index <= q_index) & (k_index.astype(F32) >= ds_wide)
    bias[...] = jnp.where(allowed, 0.0, MASKED)

    def pass_rows(j):
        own = ptile[0, pl.ds(2 * k + j, 1), :]
        other = ptile[1, pl.ds(2 * k + j, 1), :]
        return jnp.where(first, own, other), jnp.where(first, other, own)

    cl_copy.wait_recv()
    p_copy.wait_recv()
    s_copy = remote(ssend, srecv, lin_s.at[2], lin_r.at[2], nxt)
    t_copy = remote(tsend, trecv, lin_s.at[3], lin_r.at[3], nxt)
    i_copy = remote(isend, st.at[mine], lin_s.at[4], lin_r.at[4], par)
    for j in range(half):
        own, other = cl[2 * k + j], clr[j]
        x0, x1 = jnp.where(first, own, other), jnp.where(first, other, own)
        p0, p1 = pass_rows(j)
        x0b[j] = x0
        comb[j] = x1 + p1 * x0
        ssend[j] = comb[j].astype(BF16)
    s_copy.start()
    step_b(0)
    step_a(2)
    s_copy.wait_recv()
    for j in range(half):
        p0, p1 = pass_rows(j)
        tsend[j] = (comb[j] + (p1 * p0) * srecv[j].astype(F32)).astype(BF16)
    t_copy.start()
    step_b(1)
    step_a(3)
    step_c(0)
    step_d(0)

    def soft(h):
        query, cot = hb[3, h], hb[4, h]
        keys, values = kv[h, 0, window, :], kv[h, 1, window, :]
        logits = dot_nt(query, keys) * inv_root + bias[...]
        top = jnp.max(logits, axis=1, keepdims=True)
        expo = jnp.exp(logits - top)
        inverse = 1.0 / jnp.sum(expo, axis=1, keepdims=True)
        out = (dot_nn(expo.astype(BF16), values) * inverse).astype(BF16).astype(F32)
        ostage[O_SOFT, pl.ds(h, tok, stride=heads), :] = out
        delta = jnp.sum(cot.astype(F32) * out, axis=1, keepdims=True)
        probs = expo * inverse
        slopes = (inv_root * probs * (dot_nt(cot, values) - delta)).astype(BF16)
        ostage[O_SQ, pl.ds(h, tok, stride=heads), :] = dot_nn(slopes, keys)
        gacc[h, 0, window, :] = dot_tn(slopes, query)
        gacc[h, 1, window, :] = dot_tn(probs.astype(BF16), cot)

    def bwd_copy(kind, h):
        if kind == 0:
            return remote(gsend.at[h], grecv.at[h], bwd_s.at[0, h], bwd_r.at[0, h], par)
        if kind == 1:
            return remote(fsend.at[h], frecv.at[h], bwd_s.at[1, h], bwd_r.at[1, h], prv)
        return remote(nsend.at[h], nrecv.at[h], bwd_s.at[2, h], bwd_r.at[2, h], prv)

    bwd = {(kind, h): bwd_copy(kind, h) for kind in range(3) for h in range(heads)}

    def step_e(h):
        for part in range(2):
            gsend[h, 0, part] = gacc[h, part, rows(1 + k), :].astype(BF16)
            gsend[h, 1, part] = gacc[h, part, rows(3 + k), :].astype(BF16)
        bwd[0, h].start()

    def step_f(h):
        bwd[0, h].wait_recv()
        for part in range(2):
            gacc[h, part, rows(2 - k), :] += grecv[h, 0, part].astype(F32)
            gacc[h, part, rows(4 - k), :] += grecv[h, 1, part].astype(F32)
            fsend[h, part] = gacc[h, part, rows(k), :].astype(BF16)
        bwd[1, h].start()

    def step_g(h):
        bwd[1, h].wait_recv()
        for part in range(2):
            nsend[h, part] = (
                gacc[h, part, rows(2 + k), :] + frecv[h, part].astype(F32)
            ).astype(BF16)
        bwd[2, h].start()

    def step_h(h):
        bwd[2, h].wait_recv()
        for part, place in ((0, O_SK), (1, O_SV)):
            ostage[place, pl.ds(h, tok, stride=heads), :] = (
                gacc[h, part, rows(4 + k), :] + nrecv[h, part].astype(F32)
            )

    out_copies = []

    def store(i):
        obf[i] = ostage[i].astype(BF16)
        copy = pltpu.make_async_copy(obf.at[i], outs[i], out_sem.at[i])
        copy.start()
        out_copies.append(copy)

    soft(0)
    step_e(0)
    step_b(2)
    step_c(1)

    t_copy.wait_recv()
    for j in range(half):
        p0, p1 = pass_rows(j)
        in0 = trecv[j].astype(F32)
        in1 = x0b[j] + p0 * in0
        st[2 * k + j] = jnp.where(first, in0, in1).astype(BF16)
        isend[j] = jnp.where(first, in1, in0).astype(BF16)
    i_copy.start()
    step_d(1)
    step_f(0)
    soft(1)
    step_e(1)
    step_b(3)
    step_c(2)

    i_copy.wait_recv()
    squares = jnp.zeros((tok, size), F32)
    crossed = jnp.zeros((tok, size), F32)
    for h in range(heads):
        value = rawo[h] + enter[h] * dot_nn(hb[0, h], st[h])
        rawo[h] = value
        squares += value * value
        crossed += head_of(LC, h) * ngv[h : h + 1, :] * value
    ysend[0:1, :] = jnp.sum(jnp.transpose(squares), axis=0, keepdims=True)
    ysend[1:2, :] = jnp.sum(jnp.transpose(crossed), axis=0, keepdims=True)
    ysend[2:, :] = jnp.zeros((6, tok), F32)
    y_copies = []
    for step in range(1, n_head):
        y_copies.append(
            pltpu.make_async_remote_copy(
                src_ref=ysend, dst_ref=yrecv.at[step], send_sem=y_s.at[step], recv_sem=y_r.at[step],
                device_id=(me, lax.rem(hd + step, n_head)), device_id_type=MESH,
            )
        )
        y_copies[-1].start()
    step_f(1)
    step_g(0)
    step_d(2)
    soft(2)
    step_e(2)
    step_c(3)

    total = ysend[...]
    for step in range(1, n_head):
        y_copies[step - 1].wait_recv()
        total += yrecv[step]
    count = heads * size * n_head
    rscale_row = lax.rsqrt(total[0:1, :] / count + NORM_EPS)
    factor_row = rscale_row * rscale_row * rscale_row * (total[1:2, :] / count)
    rscale = jnp.transpose(jnp.broadcast_to(rscale_row, (tok, tok)))
    factor = jnp.transpose(jnp.broadcast_to(factor_row, (tok, tok)))
    for h in range(heads):
        gain = ngv[h : h + 1, :]
        value = rawo[h]
        ostage[O_LIN, pl.ds(h, tok, stride=heads), :] = value * rscale * gain
        grad = (rscale * (head_of(LC, h) * gain) - value * factor).astype(BF16)
        rgrad[h] = grad
        carried = (enter[h] * hb[0, h].astype(F32)).astype(BF16)
        pu[h] = dot_tn(carried, grad)
    pu_copy = remote(pu.at[theirs], pur, lin_s.at[5], lin_r.at[5], par)
    pu_copy.start()
    store(O_LIN)
    step_f(2)
    step_g(1)
    step_h(0)
    step_d(3)

    pu_copy.wait_recv()
    r_copy = remote(rsend, rrecv, lin_s.at[6], lin_r.at[6], prv)
    q_copy = remote(qsend, qrecv, lin_s.at[7], lin_r.at[7], prv)
    o_copy = remote(osend, back.at[mine], lin_s.at[8], lin_r.at[8], par)
    for j in range(half):
        own, other = pu[2 * k + j], pur[j]
        y0, y1 = jnp.where(first, own, other), jnp.where(first, other, own)
        p0, p1 = pass_rows(j)
        x0b[j] = y1
        comb[j] = y0 + p0 * y1
        rsend[j] = comb[j].astype(BF16)
    r_copy.start()

    soft(3)
    step_e(3)

    r_copy.wait_recv()
    for j in range(half):
        p0, p1 = pass_rows(j)
        qsend[j] = (comb[j] + (p0 * p1) * rrecv[j].astype(F32)).astype(BF16)
    q_copy.start()
    step_f(3)
    step_g(2)
    step_h(1)
    store(O_SOFT)
    store(O_SQ)

    for h in range(heads):
        query, key, value, grad = hb[0, h], hb[1, h], hb[2, h], rgrad[h]
        mixed = (within[h] * dot_nt(grad, value)).astype(BF16)
        ostage[O_LQ, pl.ds(h, tok, stride=heads), :] = dot_nn(mixed, key) + enter[h] * dot_nt(
            grad, st[h]
        )
        dkp[h] = dot_tn(mixed, query)
        dvp[h] = dot_tn(attend[h], grad)
    store(O_LQ)

    q_copy.wait_recv()
    for j in range(half):
        p0, p1 = pass_rows(j)
        out1 = qrecv[j].astype(F32)
        out0 = x0b[j] + p1 * out1
        back[2 * k + j] = jnp.where(first, out0, out1).astype(BF16)
        osend[j] = jnp.where(first, out1, out0).astype(BF16)
    o_copy.start()
    step_g(3)
    step_h(2)

    o_copy.wait_recv()
    for h in range(heads):
        ostage[O_LK, pl.ds(h, tok, stride=heads), :] = dkp[h] + leave[h] * dot_nt(
            hb[2, h], back[h]
        )
        ostage[O_LV, pl.ds(h, tok, stride=heads), :] = dvp[h] + leave[h] * dot_nn(
            hb[1, h], back[h]
        )
    store(O_LK)
    store(O_LV)
    step_h(3)
    store(O_SK)
    store(O_SV)

    for copy in list(fwd.values()) + list(bwd.values()) + y_copies:
        copy.wait_send()
    for copy in (cl_copy, p_copy, s_copy, t_copy, i_copy, pu_copy, r_copy, q_copy, o_copy):
        copy.wait_send()
    for copy in out_copies:
        copy.wait()


def write_out(*refs):
    copies = [pltpu.make_async_copy(refs[i], refs[8 + i], refs[16].at[i]) for i in range(8)]
    for copy in copies:
        copy.start()
    for copy in copies:
        copy.wait()


def shards(n_ctx, n_head, *args):
    tok, heads, size = args[0].shape
    (lq, lk, lv, ld, ng, lc, sq, sk, sv, sc, ds) = args
    flat = (tok * heads, size)
    big = [a.reshape(flat) for a in (lq, lk, lv, lc, sq, sk, sv, sc)]
    square = (heads, tok, size)
    half = (heads // 2, size, size)
    wide = (heads, 2, (SPAN + 2) * tok, size)
    vmem = pltpu.VMEM
    dma = pltpu.SemaphoreType.DMA
    any_spec = pl.BlockSpec(memory_space=pl.ANY)
    pair = (heads, 2, tok, size)
    scratch = [
        vmem((8,) + flat, BF16),
        vmem((8,) + flat, F32),
        vmem((5,) + square, BF16),
        vmem(wide, BF16),
        vmem((heads, tok), F32),
        vmem((heads, size), F32),
        vmem((1, tok), jnp.int32),
        vmem((tok, (SPAN + 1) * tok), F32),
        vmem((tok, tok), F32),
        vmem(square, F32),
        vmem(square, F32),
        vmem(square, F32),
        vmem(wide, F32),
        vmem((heads, 2, 2, tok, size), BF16),
        vmem((heads, 2, 2, tok, size), BF16),
        vmem(pair, BF16),
        vmem(pair, BF16),
        vmem(pair, BF16),
        vmem(pair, BF16),
        vmem((heads, size, size), F32),
        vmem(half, F32),
        vmem((2, 8, size), F32),
        vmem(half, F32),
        vmem(half, F32),
        vmem(half, BF16),
        vmem(half, BF16),
        vmem(half, BF16),
        vmem(half, BF16),
        vmem(half, BF16),
        vmem((heads, size, size), BF16),
        vmem((8, tok), F32),
        vmem((n_head, 8, tok), F32),
        vmem((heads, tok, tok), BF16),
        vmem(square, F32),
        vmem(square, BF16),
        vmem((heads, size, size), F32),
        vmem(half, F32),
        vmem(half, BF16),
        vmem(half, BF16),
        vmem(half, BF16),
        vmem(half, BF16),
        vmem(half, BF16),
        vmem((heads, size, size), BF16),
        vmem(square, F32),
        vmem(square, F32),
        vmem((8,) + flat, F32),
        vmem((8,) + flat, BF16),
        dma((8,)),
        dma((8,)),
        dma((3,)),
        dma((4, heads)),
        dma((4, heads)),
        dma((3, heads)),
        dma((3, heads)),
        dma((9,)),
        dma((9,)),
        dma((n_head,)),
        dma((n_head,)),
    ]
    results = pl.pallas_call(
        functools.partial(kernel, n_ctx, n_head, heads, tok, size),
        out_shape=[vmem(flat, BF16)] * 8,
        in_specs=[any_spec] * 11,
        out_specs=[any_spec] * 8,
        scratch_shapes=scratch,
        compiler_params=pltpu.CompilerParams(
            collective_id=0, has_side_effects=True, vmem_limit_bytes=48 * 1024 * 1024
        ),
    )(*[pltpu.with_memory_space_constraint(a, pltpu.HBM) for a in (*big, ld, ng, ds.reshape(1, tok))])
    results = pl.pallas_call(
        write_out,
        out_shape=[jax.ShapeDtypeStruct(flat, BF16)] * 8,
        in_specs=[any_spec] * 8,
        out_specs=[any_spec] * 8,
        scratch_shapes=[dma((8,))],
    )(*[pltpu.with_memory_space_constraint(r, pltpu.VMEM) for r in results])
    return tuple(r.reshape(tok, heads, size) for r in results)


def solution(mesh):
    cube = P("ctx", "head", None)
    in_specs = (
        cube, cube, cube, P("head", "ctx"), P("head", None), cube, cube, cube, cube, cube, P("ctx"),
    )
    return jax.shard_map(
        functools.partial(shards, mesh.shape["ctx"], mesh.shape["head"]),
        mesh=mesh, in_specs=in_specs, out_specs=(cube,) * 8, check_vma=False,
    )
```

time: 132 us -> 50.1 us (0.38)
  the two profiles are of different devices: /device:TPU:7 before, /device:TPU:1 now
where the time goes in v1:
time: 50.1 us; the launch traced here: 49.9 us
  Pallas kernels  49.3 us (98%)
  between operations  0.65 us (1%)
    pallas_call x1, Pallas kernels, shards(): pl.pallas_call(functools.partial(kernel, n_ctx, n_head, heads, tok, size)...  48.3 us
    pallas_call x1, Pallas kernels, shards(): pl.pallas_call(write_out, out_shape=[jax.ShapeDtypeStruct(flat, BF16)] *...  1.03 us

profile of v1, /device:TPU:1, one launch (start us, length us, event | category | flops | bytes accessed | tf_op | source)
XLA Modules:
  0.0 49.9 jit_solution(8842284420975930653)
XLA Ops:
  0.6 48.3 %shard_map.170 = (bf16[512,128]{1,0:T(8,128)(2,1)S(1)}, bf16[512,128]{1,0:T(8,128)(2,1)S(1)}, bf16[512,128]{1,0:T(8,128)(2,1)S(1)}, bf16[512,128]{1,0:T(8,128)(2...) custom-call(bf16[512,128]{1,0:T(8,128)(2,1)} %bitcast.17, ...), custom_call_target="tpu_custom_call" | custom-call | tf_op jit(solution)/shard_map/pallas_call | solution.py:510
  48.9 1.0 %shard_map.171 = (bf16[512,128]{1,0:T(8,128)(2,1)}, bf16[512,128]{1,0:T(8,128)(2,1)}, bf16[512,128]{1,0:T(8,128)(2,1)}, bf16[512,128]{1,0:T(8,128)(2,1)}, bf16[5...) custom-call(bf16[512,128]{1,0:T(8,128)(2,1)S(1)} %get-tuple-element.24.refs_, ...), custom_call_target="tpu_custom_call" | custom-call | tf_op jit(solution)/shard_map/pallas_call | solution.py:520

commit v2 on v0

v2 whole, which is shorter than its diff:
```python
import functools
import math

import jax
import jax.numpy as jnp
from jax import lax
from jax.experimental import pallas as pl
from jax.experimental.pallas import tpu as pltpu
from jax.sharding import PartitionSpec as P

SPAN = 4
NORM_EPS = 1e-05
MASKED = -1e30
MESH = pl.DeviceIdType.MESH
F32 = jnp.float32
BF16 = jnp.bfloat16

LQ, LK, LV, LC, SQ, SK, SV, SC = range(8)
O_LIN, O_LQ, O_LK, O_LV, O_SOFT, O_SQ, O_SK, O_SV = range(8)


DIRECT_KV = ()


def dot_nn(a, b):
    return lax.dot_general(a, b, (((1,), (0,)), ((), ())), preferred_element_type=F32)


def dot_nt(a, b):
    return lax.dot_general(a, b, (((1,), (1,)), ((), ())), preferred_element_type=F32)


def dot_tn(a, b):
    return lax.dot_general(a, b, (((0,), (0,)), ((), ())), preferred_element_type=F32)


def kernel(n_ctx, n_head, heads, tok, size, *refs):
    ins = refs[:8]
    ld_in, ng_in, ds_in = refs[8:11]
    outs = refs[11:19]
    (
        raw, stage, hb, kv, ldv, ngv, dsv, bias, bias_t, mask, enter, leave, within,
        qd, stats,
        cl, clr, ptile, pprod, x0b, comb, ssend, snear, tsend, sfar, isend, st,
        ysend, yrecv, attend, rawo, rgrad, pu, pur, rsend, rnear, rfar, osend, back,
        dkp, dvp, ostage,
        in_sem, small_sem, fwd_s, fwd_r, bwd_s, bwd_r, st_s, st_r, lin_s, lin_r, y_s, y_r,
    ) = refs[19:]
    half = heads // 2
    span = SPAN * tok
    width = span + tok
    me = lax.axis_index("ctx")
    hd = lax.axis_index("head")
    k = lax.rem(me, 2)
    first = k == 0
    par = me + 1 - 2 * k
    nxt = lax.rem(me + 2, n_ctx)
    prv = lax.rem(me + n_ctx - 2, n_ctx)
    nxt2 = lax.rem(me + 4, n_ctx)
    prv2 = lax.rem(me + n_ctx - 4, n_ctx)
    inv_root = 1.0 / math.sqrt(size)

    def window(ref, h, part):
        return ref[h, pl.ds(k, SPAN + 1), part].reshape(width, size)

    mine = pl.ds(2 * k, half)
    theirs = pl.ds(2 * (1 - k), half)

    copies = {}

    def remote(name, src, dst, send, recv, where):
        copies[name] = pltpu.make_async_remote_copy(
            src_ref=src, dst_ref=dst, send_sem=send, recv_sem=recv,
            device_id=where, device_id_type=MESH,
        )

    barrier = pltpu.get_barrier_semaphore()
    before = [lax.rem(me + n_ctx - step, n_ctx) for step in range(1, SPAN + 1)]
    after = [lax.rem(me + step, n_ctx) for step in range(1, SPAN + 1)]
    for other in before + after:
        pl.semaphore_signal(barrier, inc=1, device_id=(other, hd), device_id_type=MESH)
    peers = [(me, lax.rem(hd + step, n_head)) for step in range(1, n_head)]
    for peer in peers:
        pl.semaphore_signal(barrier, inc=1, device_id=peer, device_id_type=MESH)

    loads = [pltpu.make_async_copy(ins[i], raw.at[i], in_sem.at[i]) for i in range(8)]
    small = [
        pltpu.make_async_copy(ds_in, dsv, small_sem.at[0]),
        pltpu.make_async_copy(ld_in, ldv, small_sem.at[1]),
        pltpu.make_async_copy(ng_in, ngv, small_sem.at[2]),
    ]
    for copy in small:
        copy.start()
    for i in (LK, LV, SK, SV):
        loads[i].start()
    for i in (SQ, SC, LQ, LC):
        loads[i].start()

    for h in range(heads):
        whole = kv.at[h]

        def block(slot):
            return whole.at[slot]

        sems = [(fwd_s.at[kind, h], fwd_r.at[kind, h]) for kind in range(4)]
        remote(("near", h), block(4 + k), block(2 + k), *sems[0], (nxt, hd))
        if h in DIRECT_KV:
            remote(("far", h), block(4 + k), block(k), *sems[1], (nxt2, hd))
        else:
            remote(("far", h), block(2 + k), block(k), *sems[1], (nxt, hd))
        remote(("core", h), block(4 - k), block(4 - k), *sems[2], (par, hd))
        remote(("core2", h), block(2 - k), block(2 - k), *sems[3], (par, hd))
        queries = qd.at[h]

        def qblock(slot):
            return queries.at[slot]

        sems = [(bwd_s.at[kind, h], bwd_r.at[kind, h]) for kind in range(4)]
        remote(("qnear", h), qblock(k), qblock(2 + k), *sems[0], (prv, hd))
        remote(("qfar", h), qblock(2 + k), qblock(4 + k), *sems[1], (prv, hd))
        remote(("qcore", h), qblock(2 - k), qblock(2 - k), *sems[2], (par, hd))
        remote(("qcore2", h), qblock(4 - k), qblock(4 - k), *sems[3], (par, hd))
        for i in range(SPAN):
            remote(
                ("stats", h, i), stats.at[h, 0], stats.at[h, i + 1],
                st_s.at[i, h], st_r.at[i, h], (before[i], hd),
            )
    lin = [
        ("closing", cl.at[theirs], clr, par),
        ("pass", ptile.at[0], ptile.at[1], par),
        ("pprev", pprod.at[0], pprod.at[1], prv),
        ("snear", ssend, snear, nxt),
        ("sfar", tsend, sfar, nxt),
        ("state", isend, st.at[mine], par),
        ("pulled", pu.at[theirs], pur, par),
        ("rnear", rsend, rnear, prv),
        ("rfar", rsend, rfar, prv2),
        ("back", osend, back.at[mine], par),
    ]
    for i, (name, src, dst, where) in enumerate(lin):
        remote(name, src, dst, lin_s.at[i], lin_r.at[i], (where, hd))
    for step, peer in enumerate(peers):
        remote(("sums", step), ysend, yrecv.at[step], y_s.at[step], y_r.at[step], peer)

    def head_of(i, h):
        return stage[i, pl.ds(h, tok, stride=heads), :]

    def unpack(i, place):
        loads[i].wait()
        stage[i] = raw[i].astype(F32)
        for h in range(heads):
            if place is not None:
                hb[place, h] = head_of(i, h).astype(BF16)

    def put(place, h, value):
        ostage[place, pl.ds(h, tok, stride=heads), :] = value

    def finish(place):
        outs[place][...] = ostage[place].astype(BF16)

    def pass_rows(j):
        own = ptile[0, pl.ds(2 * k + j, 1), :]
        other = ptile[1, pl.ds(2 * k + j, 1), :]
        return jnp.where(first, own, other), jnp.where(first, other, own)

    def load_kv():
        for i, part in ((SK, 0), (SV, 1)):
            loads[i].wait()
            stage[i] = raw[i].astype(F32)
            for h in range(heads):
                kv[h, 4 + k, part] = head_of(i, h).astype(BF16)

    def load_qd():
        for i, part in ((SQ, 0), (SC, 1)):
            loads[i].wait()
            stage[i] = raw[i].astype(F32)
            for h in range(heads):
                qd[h, k, part] = head_of(i, h).astype(BF16)

    def send_qd(h):
        copies["qnear", h].start()

    def qrelay(h):
        copies["qnear", h].wait_recv()
        copies["qfar", h].start()
        copies["qcore", h].start()

    def qrelay_core(h):
        copies["qfar", h].wait_recv()
        copies["qcore2", h].start()

    def enter_kernel():
        pl.semaphore_wait(barrier, 2 * SPAN + n_head - 1)

    def send_own(h):
        copies["near", h].start()
        if h in DIRECT_KV:
            copies["far", h].start()

    def relay(h):
        copies["near", h].wait_recv()
        if h not in DIRECT_KV:
            copies["far", h].start()
        copies["core", h].start()

    def relay_core(h):
        copies["far", h].wait_recv()
        copies["core2", h].start()

    def soft(h):
        copies["core", h].wait_recv()
        copies["core2", h].wait_recv()
        query, cot = qd[h, k, 0], qd[h, k, 1]
        keys, values = window(kv, h, 0), window(kv, h, 1)
        logits = dot_nt(query, keys) * inv_root + bias[...]
        top = jnp.max(logits, axis=1, keepdims=True)
        expo = jnp.exp(logits - top)
        total = jnp.sum(expo, axis=1, keepdims=True)
        inverse = 1.0 / total
        out = (dot_nn(expo.astype(BF16), values) * inverse).astype(BF16).astype(F32)
        put(O_SOFT, h, out)
        delta = jnp.sum(cot.astype(F32) * out, axis=1, keepdims=True)
        lane = lax.broadcasted_iota(jnp.int32, (tok, tok), 1)
        figures = jnp.where(lane == 0, top + jnp.log(total), jnp.where(lane == 1, delta, mask[1]))
        stats[h, 0] = jnp.transpose(figures)[:8, :]
        for i in range(SPAN):
            copies["stats", h, i].start()
        slopes = inv_root * (expo * inverse) * (dot_nt(cot, values) - delta)
        put(O_SQ, h, dot_nn(slopes.astype(BF16), keys))

    def soft_grad(h):
        copies["qcore", h].wait_recv()
        copies["qcore2", h].wait_recv()
        if h > 0:
            for i in range(SPAN):
                copies["stats", h, i].wait_recv()
        keys, values = kv[h, 4 + k, 0], kv[h, 4 + k, 1]
        queries, cots = window(qd, h, 0), window(qd, h, 1)
        wide = [
            jnp.concatenate([stats[h, i, row : row + 1, :] for i in range(SPAN + 1)], axis=1)
            for row in range(2)
        ]
        logits = dot_nt(keys, queries) * inv_root + bias_t[...]
        probs = jnp.exp(logits - wide[0])
        put(O_SV, h, dot_nn(probs.astype(BF16), cots))
        slopes = inv_root * probs * (dot_nt(values, cots) - wide[1])
        put(O_SK, h, dot_nn(slopes.astype(BF16), queries))

    def later_mask():
        for i in range(SPAN):
            copies["stats", 0, i].wait_recv()
        k_index = lax.broadcasted_iota(jnp.int32, (tok, width), 0)
        q_index = lax.broadcasted_iota(jnp.int32, (tok, width), 1)
        starts = jnp.concatenate([stats[0, i, 2:3, :] for i in range(SPAN + 1)], axis=1)
        position = k_index.astype(F32) + (me * tok).astype(F32)
        inside = q_index < (n_ctx - me) * tok
        allowed = (k_index <= q_index) & (position >= starts) & inside
        bias_t[...] = jnp.where(allowed, 0.0, MASKED)

    def decays():
        for copy in small:
            copy.wait()
        t_pos = lax.broadcasted_iota(jnp.int32, (tok, tok), 0)
        s_pos = lax.broadcasted_iota(jnp.int32, (tok, tok), 1)
        first_row = (me * tok).astype(F32)
        ds_row = jnp.broadcast_to(dsv[...].astype(F32), (tok, tok))
        ds_col = jnp.transpose(ds_row)
        mask[0] = jnp.where((ds_row == ds_col) & (s_pos <= t_pos), 1.0, 0.0)
        mask[1] = ds_col
        ds_last = jnp.broadcast_to(ds_row[:, tok - 1 :], (tok, tok))
        triangle = jnp.where(t_pos <= s_pos, 1.0, 0.0).astype(F32)
        logs = jnp.concatenate([ldv[...], jnp.zeros((8 - heads, tok), F32)], axis=0)
        cumulative = lax.dot_general(
            logs, triangle, (((1,), (0,)), ((), ())),
            precision=lax.Precision.HIGHEST, preferred_element_type=F32,
        )
        for h in range(heads):
            cum_row = jnp.broadcast_to(cumulative[h : h + 1, :], (tok, tok))
            cum_col = jnp.transpose(cum_row)
            gap = jnp.exp(jnp.minimum(cum_col - cum_row, 0.0))
            within[h] = jnp.where(mask[0] > 0.0, gap, 0.0)
            enter[h] = jnp.where(ds_col < first_row, jnp.exp(cum_col), 0.0)
            cum_last = jnp.broadcast_to(cum_row[:, tok - 1 :], (tok, tok))
            leave[h] = jnp.where(ds_col == ds_last, jnp.exp(cum_last - cum_col), 0.0)
            ptile[0, h : h + 1, :] = enter[h, tok - 1 :, :]
        ptile[0, heads:, :] = jnp.zeros((8 - heads, size), F32)

    def closing():
        unpack(LK, 1)
        unpack(LV, 2)
        for h in range(heads):
            keyed = (leave[h] * head_of(LK, h)).astype(BF16)
            cl[h] = dot_tn(keyed, hb[2, h])

    def send_closing():
        copies["closing"].start()
        copies["pass"].start()

    def local_lin():
        unpack(LQ, 0)
        for h in range(heads):
            attend[h] = (within[h] * dot_nt(hb[0, h], hb[1, h])).astype(BF16)
            rawo[h] = dot_nn(attend[h], hb[2, h])
        unpack(LC, None)

    def local_soft():
        q_index = lax.broadcasted_iota(jnp.int32, (tok, width), 0) + span
        k_index = lax.broadcasted_iota(jnp.int32, (tok, width), 1)
        starts = jnp.concatenate([mask[1]] * (width // tok), axis=1)
        position = k_index.astype(F32) + (me * tok - span).astype(F32)
        allowed = (k_index <= q_index) & (position >= starts)
        bias[...] = jnp.where(allowed, 0.0, MASKED)

    def state_send():
        copies["pass"].wait_recv()
        pprod[0] = ptile[0] * ptile[1]
        copies["closing"].wait_recv()
        for j in range(half):
            own, other = cl[2 * k + j], clr[j]
            x0, x1 = jnp.where(first, own, other), jnp.where(first, other, own)
            p0, p1 = pass_rows(j)
            x0b[j] = x0
            comb[j] = x1 + p1 * x0
            ssend[j] = comb[j].astype(BF16)
        copies["snear"].start()
        copies["pprev"].start()

    def state_relay():
        copies["snear"].wait_recv()
        for j in range(half):
            both = pprod[0, pl.ds(2 * k + j, 1), :]
            tsend[j] = (comb[j] + both * snear[j].astype(F32)).astype(BF16)
        copies["sfar"].start()

    def state_get():
        copies["sfar"].wait_recv()
        for j in range(half):
            p0, p1 = pass_rows(j)
            in0 = sfar[j].astype(F32)
            in1 = x0b[j] + p0 * in0
            st[2 * k + j] = jnp.where(first, in0, in1).astype(BF16)
            isend[j] = jnp.where(first, in1, in0).astype(BF16)
        copies["state"].start()

    def lin_raw():
        copies["state"].wait_recv()
        squares = jnp.zeros((tok, size), F32)
        crossed = jnp.zeros((tok, size), F32)
        for h in range(heads):
            value = rawo[h] + enter[h] * dot_nn(hb[0, h], st[h])
            rawo[h] = value
            squares += value * value
            crossed += head_of(LC, h) * ngv[h : h + 1, :] * value
        ysend[0:1, :] = jnp.sum(jnp.transpose(squares), axis=0, keepdims=True)
        ysend[1:2, :] = jnp.sum(jnp.transpose(crossed), axis=0, keepdims=True)
        ysend[2:, :] = jnp.zeros((6, tok), F32)
        for step in range(n_head - 1):
            copies["sums", step].start()

    def lin_norm():
        total = ysend[...]
        for step in range(n_head - 1):
            copies["sums", step].wait_recv()
            total += yrecv[step]
        count = heads * size * n_head
        rscale_row = lax.rsqrt(total[0:1, :] / count + NORM_EPS)
        factor_row = rscale_row * rscale_row * rscale_row * (total[1:2, :] / count)
        rscale = jnp.transpose(jnp.broadcast_to(rscale_row, (tok, tok)))
        factor = jnp.transpose(jnp.broadcast_to(factor_row, (tok, tok)))
        for h in range(heads):
            gain = ngv[h : h + 1, :]
            value = rawo[h]
            put(O_LIN, h, value * rscale * gain)
            grad = (rscale * (head_of(LC, h) * gain) - value * factor).astype(BF16)
            rgrad[h] = grad
            carried = (enter[h] * hb[0, h].astype(F32)).astype(BF16)
            pu[h] = dot_tn(carried, grad)
        copies["pulled"].start()

    def back_send():
        copies["pulled"].wait_recv()
        for j in range(half):
            own, other = pu[2 * k + j], pur[j]
            y0, y1 = jnp.where(first, own, other), jnp.where(first, other, own)
            p0, p1 = pass_rows(j)
            x0b[j] = y1
            rsend[j] = (y0 + p0 * y1).astype(BF16)
        copies["rnear"].start()
        copies["rfar"].start()

    def back_get():
        for name in ("rnear", "rfar", "pprev"):
            copies[name].wait_recv()
        for j in range(half):
            p0, p1 = pass_rows(j)
            out1 = rnear[j].astype(F32) + pprod[1, pl.ds(2 * k + j, 1), :] * rfar[j].astype(F32)
            out0 = x0b[j] + p1 * out1
            back[2 * k + j] = jnp.where(first, out0, out1).astype(BF16)
            osend[j] = jnp.where(first, out1, out0).astype(BF16)
        copies["back"].start()

    def lin_local_grads():
        for h in range(heads):
            query, key, value, grad = hb[0, h], hb[1, h], hb[2, h], rgrad[h]
            mixed = (within[h] * dot_nt(grad, value)).astype(BF16)
            put(O_LQ, h, dot_nn(mixed, key) + enter[h] * dot_nt(grad, st[h]))
            dkp[h] = dot_tn(mixed, query)
            dvp[h] = dot_tn(attend[h], grad)

    def lin_grads():
        copies["back"].wait_recv()
        for h in range(heads):
            put(O_LK, h, dkp[h] + leave[h] * dot_nt(hb[2, h], back[h]))
            put(O_LV, h, dvp[h] + leave[h] * dot_nn(hb[1, h], back[h]))

    decays()
    closing()
    enter_kernel()
    send_closing()
    load_kv()
    send_own(0)
    load_qd()
    send_qd(0)
    send_qd(1)
    local_lin()
    state_send()
    send_own(1)
    send_qd(2)
    local_soft()
    relay(0)
    send_own(2)
    state_relay()
    send_qd(3)
    relay(1)
    send_own(3)
    qrelay(0)
    qrelay(1)
    qrelay(2)
    state_get()
    relay(2)
    qrelay(3)
    relay_core(0)
    lin_raw()
    relay(3)
    relay_core(1)
    soft(0)
    qrelay_core(0)
    qrelay_core(1)
    relay_core(2)
    soft(1)
    qrelay_core(2)
    lin_norm()
    relay_core(3)
    soft(2)
    back_send()
    qrelay_core(3)
    soft(3)
    later_mask()
    soft_grad(0)
    finish(0)
    finish(4)
    finish(5)
    lin_local_grads()
    finish(1)
    soft_grad(1)
    soft_grad(2)
    back_get()
    soft_grad(3)
    finish(6)
    finish(7)
    lin_grads()
    finish(2)
    finish(3)
    for copy in copies.values():
        copy.wait_send()


def write_out(*refs):
    copies = [pltpu.make_async_copy(refs[i], refs[8 + i], refs[16].at[i]) for i in range(8)]
    for copy in copies:
        copy.start()
    for copy in copies:
        copy.wait()


def shards(n_ctx, n_head, *args):
    tok, heads, size = args[0].shape
    (lq, lk, lv, ld, ng, lc, sq, sk, sv, sc, ds) = args
    flat = (tok * heads, size)
    big = [a.reshape(flat) for a in (lq, lk, lv, lc, sq, sk, sv, sc)]
    square = (heads, tok, size)
    half = (heads // 2, size, size)
    wide = (heads, SPAN + 2, 2, tok, size)
    vmem = pltpu.VMEM
    dma = pltpu.SemaphoreType.DMA
    any_spec = pl.BlockSpec(memory_space=pl.ANY)
    pair = (heads, 2, tok, size)
    scratch = [
        vmem((8,) + flat, BF16),
        vmem((8,) + flat, F32),
        vmem((3,) + square, BF16),
        vmem(wide, BF16),
        vmem((heads, tok), F32),
        vmem((heads, size), F32),
        vmem((1, tok), jnp.int32),
        vmem((tok, (SPAN + 1) * tok), F32),
        vmem((tok, (SPAN + 1) * tok), F32),
        vmem((2, tok, tok), F32),
        vmem(square, F32),
        vmem(square, F32),
        vmem(square, F32),
        vmem(wide, BF16),
        vmem((heads, SPAN + 1, 8, tok), F32),
        vmem((heads, size, size), F32),
        vmem(half, F32),
        vmem((2, 8, size), F32),
        vmem((2, 8, size), F32),
        vmem(half, F32),
        vmem(half, F32),
        vmem(half, BF16),
        vmem(half, BF16),
        vmem(half, BF16),
        vmem(half, BF16),
        vmem(half, BF16),
        vmem((heads, size, size), BF16),
        vmem((8, tok), F32),
        vmem((n_head, 8, tok), F32),
        vmem((heads, tok, tok), BF16),
        vmem(square, F32),
        vmem(square, BF16),
        vmem((heads, size, size), F32),
        vmem(half, F32),
        vmem(half, BF16),
        vmem(half, BF16),
        vmem(half, BF16),
        vmem(half, BF16),
        vmem((heads, size, size), BF16),
        vmem(square, F32),
        vmem(square, F32),
        vmem((8,) + flat, F32),
        dma((8,)),
        dma((3,)),
        dma((4, heads)),
        dma((4, heads)),
        dma((4, heads)),
        dma((4, heads)),
        dma((SPAN, heads)),
        dma((SPAN, heads)),
        dma((10,)),
        dma((10,)),
        dma((n_head,)),
        dma((n_head,)),
    ]
    results = pl.pallas_call(
        functools.partial(kernel, n_ctx, n_head, heads, tok, size),
        out_shape=[vmem(flat, BF16)] * 8,
        in_specs=[any_spec] * 11,
        out_specs=[pl.BlockSpec(memory_space=pltpu.VMEM)] * 8,
        scratch_shapes=scratch,
        compiler_params=pltpu.CompilerParams(
            collective_id=0, has_side_effects=True, vmem_limit_bytes=48 * 1024 * 1024
        ),
    )(*[pltpu.with_memory_space_constraint(a, pltpu.HBM) for a in (*big, ld, ng, ds.reshape(1, tok))])
    results = pl.pallas_call(
        write_out,
        out_shape=[jax.ShapeDtypeStruct(flat, BF16)] * 8,
        in_specs=[any_spec] * 8,
        out_specs=[any_spec] * 8,
        scratch_shapes=[dma((8,))],
    )(*[pltpu.with_memory_space_constraint(r, pltpu.VMEM) for r in results])
    return tuple(r.reshape(tok, heads, size) for r in results)


def solution(mesh):
    cube = P("ctx", "head", None)
    in_specs = (
        cube, cube, cube, P("head", "ctx"), P("head", None), cube, cube, cube, cube, cube, P("ctx"),
    )
    return jax.shard_map(
        functools.partial(shards, mesh.shape["ctx"], mesh.shape["head"]),
        mesh=mesh, in_specs=in_specs, out_specs=(cube,) * 8, check_vma=False,
    )
```

time: 132 us -> 46.3 us (0.35)
  the two profiles are of different devices: /device:TPU:7 before, /device:TPU:1 now
where the time goes in v2:
time: 46.3 us; the launch traced here: 46.1 us
  Pallas kernels  45.5 us (98%)
  between operations  0.65 us (1%)
    pallas_call x1, Pallas kernels, shards(): pl.pallas_call(functools.partial(kernel, n_ctx, n_head, heads, tok, size)...  44.4 us
    pallas_call x1, Pallas kernels, shards(): pl.pallas_call(write_out, out_shape=[jax.ShapeDtypeStruct(flat, BF16)] *...  1.03 us

profile of v2, /device:TPU:1, one launch (start us, length us, event | category | flops | bytes accessed | tf_op | source)
XLA Modules:
  0.0 46.1 jit_solution(10349379279712237603)
XLA Ops:
  0.6 44.4 %shard_map.170 = (bf16[512,128]{1,0:T(8,128)(2,1)S(1)}, bf16[512,128]{1,0:T(8,128)(2,1)S(1)}, bf16[512,128]{1,0:T(8,128)(2,1)S(1)}, bf16[512,128]{1,0:T(8,128)(2...) custom-call(bf16[512,128]{1,0:T(8,128)(2,1)} %bitcast.17, ...), custom_call_target="tpu_custom_call" | custom-call | tf_op jit(solution)/shard_map/pallas_call | solution.py:554
  45.1 1.0 %shard_map.171 = (bf16[512,128]{1,0:T(8,128)(2,1)}, bf16[512,128]{1,0:T(8,128)(2,1)}, bf16[512,128]{1,0:T(8,128)(2,1)}, bf16[512,128]{1,0:T(8,128)(2,1)}, bf16[5...) custom-call(bf16[512,128]{1,0:T(8,128)(2,1)S(1)} %get-tuple-element.24.refs_, ...), custom_call_target="tpu_custom_call" | custom-call | tf_op jit(solution)/shard_map/pallas_call | solution.py:564

commit v3 on v2

--- a/solution.py
+++ b/solution.py
@@ -17,9 +17,6 @@
 
 LQ, LK, LV, LC, SQ, SK, SV, SC = range(8)
 O_LIN, O_LQ, O_LK, O_LV, O_SOFT, O_SQ, O_SK, O_SV = range(8)
-
-
-DIRECT_KV = ()
 
 
 def dot_nn(a, b):
@@ -42,9 +39,9 @@
         raw, stage, hb, kv, ldv, ngv, dsv, bias, bias_t, mask, enter, leave, within,
         qd, stats,
         cl, clr, ptile, pprod, x0b, comb, ssend, snear, tsend, sfar, isend, st,
-        ysend, yrecv, attend, rawo, rgrad, pu, pur, rsend, rnear, rfar, osend, back,
+        ysend, yrecv, attend, rawo, rgrad, pu, pur, rsend, rnear, qsend, rfar, osend, back,
         dkp, dvp, ostage,
-        in_sem, small_sem, fwd_s, fwd_r, bwd_s, bwd_r, st_s, st_r, lin_s, lin_r, y_s, y_r,
+        in_sem, small_sem, v_r, fwd_s, fwd_r, bwd_s, bwd_r, st_s, st_r, lin_s, lin_r, hop_s, hop_r, y_s, y_r,
     ) = refs[19:]
     half = heads // 2
     span = SPAN * tok
@@ -56,8 +53,6 @@
     par = me + 1 - 2 * k
     nxt = lax.rem(me + 2, n_ctx)
     prv = lax.rem(me + n_ctx - 2, n_ctx)
-    nxt2 = lax.rem(me + 4, n_ctx)
-    prv2 = lax.rem(me + n_ctx - 4, n_ctx)
     inv_root = 1.0 / math.sqrt(size)
 
     def window(ref, h, part):
@@ -102,12 +97,16 @@
         def block(slot):
             return whole.at[slot]
 
-        sems = [(fwd_s.at[kind, h], fwd_r.at[kind, h]) for kind in range(4)]
-        remote(("near", h), block(4 + k), block(2 + k), *sems[0], (nxt, hd))
-        if h in DIRECT_KV:
-            remote(("far", h), block(4 + k), block(k), *sems[1], (nxt2, hd))
+        sems = [(fwd_s.at[kind], fwd_r.at[kind, h]) for kind in range(4)]
+        if h > 0:
+            remote(("near", h), block(4 + k), block(2 + k), *sems[0], (nxt, hd))
         else:
-            remote(("far", h), block(2 + k), block(k), *sems[1], (nxt, hd))
+            for part in range(2):
+                remote(
+                    ("near", h, part), block(4 + k).at[part], block(2 + k).at[part],
+                    fwd_s.at[0], (fwd_r.at[0, 0], v_r.at[0])[part], (nxt, hd),
+                )
+        remote(("far", h), block(2 + k), block(k), *sems[1], (nxt, hd))
         remote(("core", h), block(4 - k), block(4 - k), *sems[2], (par, hd))
         remote(("core2", h), block(2 - k), block(2 - k), *sems[3], (par, hd))
         queries = qd.at[h]
@@ -115,7 +114,7 @@
         def qblock(slot):
             return queries.at[slot]
 
-        sems = [(bwd_s.at[kind, h], bwd_r.at[kind, h]) for kind in range(4)]
+        sems = [(bwd_s.at[kind], bwd_r.at[kind, h]) for kind in range(4)]
         remote(("qnear", h), qblock(k), qblock(2 + k), *sems[0], (prv, hd))
         remote(("qfar", h), qblock(2 + k), qblock(4 + k), *sems[1], (prv, hd))
         remote(("qcore", h), qblock(2 - k), qblock(2 - k), *sems[2], (par, hd))
@@ -123,24 +122,46 @@
         for i in range(SPAN):
             remote(
                 ("stats", h, i), stats.at[h, 0], stats.at[h, i + 1],
-                st_s.at[i, h], st_r.at[i, h], (before[i], hd),
+                st_s.at[0], st_r.at[h], (before[i], hd),
             )
     lin = [
         ("closing", cl.at[theirs], clr, par),
         ("pass", ptile.at[0], ptile.at[1], par),
-        ("pprev", pprod.at[0], pprod.at[1], prv),
-        ("snear", ssend, snear, nxt),
-        ("sfar", tsend, sfar, nxt),
         ("state", isend, st.at[mine], par),
         ("pulled", pu.at[theirs], pur, par),
-        ("rnear", rsend, rnear, prv),
-        ("rfar", rsend, rfar, prv2),
         ("back", osend, back.at[mine], par),
     ]
     for i, (name, src, dst, where) in enumerate(lin):
         remote(name, src, dst, lin_s.at[i], lin_r.at[i], (where, hd))
+    for j in range(half):
+        hops = [
+            ("s", ssend, snear, nxt), ("t", tsend, sfar, nxt),
+            ("r", rsend, rnear, prv), ("q", qsend, rfar, prv),
+        ]
+        for i, (name, src, dst, where) in enumerate(hops):
+            remote(
+                (name, j), src.at[j], dst.at[j], hop_s.at[i], hop_r.at[i, j], (where, hd)
+            )
     for step, peer in enumerate(peers):
-        remote(("sums", step), ysend, yrecv.at[step], y_s.at[step], y_r.at[step], peer)
+        remote(("sums", step), ysend, yrecv.at[step], y_s.at[0], y_r.at[0], peer)
+
+    def all_of(name, src, dst, send, recv):
+        remote(name, src, dst, send, recv, (par, hd))
+
+    for kind, (src, dst) in enumerate(((4 + k, 2 + k), (2 + k, k), (4 - k, 4 - k), (2 - k, 2 - k))):
+        all_of(("all", kind), kv.at[:, src], kv.at[:, dst], fwd_s.at[kind], fwd_r.at[kind, 0])
+    for kind, (src, dst) in enumerate(((k, 2 + k), (2 + k, 4 + k), (2 - k, 2 - k), (4 - k, 4 - k))):
+        all_of(("all", 4 + kind), qd.at[:, src], qd.at[:, dst], bwd_s.at[kind], bwd_r.at[kind, 0])
+    later = pl.ds(1, SPAN)
+    all_of(("all", 8), stats.at[:, later], stats.at[:, later], st_s.at[0], st_r.at[0])
+    for h in range(heads):
+        all_of(("figures", h), stats.at[h, later], stats.at[h, later], st_s.at[0], st_r.at[h])
+    others = yrecv.at[pl.ds(0, n_head - 1)]
+    all_of(("all", 9), others, others, y_s.at[0], y_r.at[0])
+    for i, (src, dst) in enumerate(
+        ((ssend, snear), (tsend, sfar), (rsend, rnear), (qsend, rfar))
+    ):
+        all_of(("all", 10 + i), src, dst, hop_s.at[i], hop_r.at[i, 0])
 
     def head_of(i, h):
         return stage[i, pl.ds(h, tok, stride=heads), :]
@@ -194,13 +215,17 @@
 
     def send_own(h):
         copies["near", h].start()
-        if h in DIRECT_KV:
-            copies["far", h].start()
+
+    def send_first(part):
+        copies["near", 0, part].start()
 
     def relay(h):
-        copies["near", h].wait_recv()
-        if h not in DIRECT_KV:
-            copies["far", h].start()
+        if h > 0:
+            copies["near", h].wait_recv()
+        else:
+            copies["near", 0, 0].wait_recv()
+            copies["near", 0, 1].wait_recv()
+        copies["far", h].start()
         copies["core", h].start()
 
     def relay_core(h):
@@ -232,8 +257,7 @@
         copies["qcore", h].wait_recv()
         copies["qcore2", h].wait_recv()
         if h > 0:
-            for i in range(SPAN):
-                copies["stats", h, i].wait_recv()
+            copies["figures", h].wait_recv()
         keys, values = kv[h, 4 + k, 0], kv[h, 4 + k, 1]
         queries, cots = window(qd, h, 0), window(qd, h, 1)
         wide = [
@@ -247,8 +271,7 @@
         put(O_SK, h, dot_nn(slopes.astype(BF16), queries))
 
     def later_mask():
-        for i in range(SPAN):
-            copies["stats", 0, i].wait_recv()
+        copies["figures", 0].wait_recv()
         k_index = lax.broadcasted_iota(jnp.int32, (tok, width), 0)
         q_index = lax.broadcasted_iota(jnp.int32, (tok, width), 1)
         starts = jnp.concatenate([stats[0, i, 2:3, :] for i in range(SPAN + 1)], axis=1)
@@ -322,19 +345,18 @@
             x0b[j] = x0
             comb[j] = x1 + p1 * x0
             ssend[j] = comb[j].astype(BF16)
-        copies["snear"].start()
-        copies["pprev"].start()
+            copies["s", j].start()
 
     def state_relay():
-        copies["snear"].wait_recv()
         for j in range(half):
+            copies["s", j].wait_recv()
             both = pprod[0, pl.ds(2 * k + j, 1), :]
             tsend[j] = (comb[j] + both * snear[j].astype(F32)).astype(BF16)
-        copies["sfar"].start()
+            copies["t", j].start()
 
     def state_get():
-        copies["sfar"].wait_recv()
         for j in range(half):
+            copies["t", j].wait_recv()
             p0, p1 = pass_rows(j)
             in0 = sfar[j].astype(F32)
             in1 = x0b[j] + p0 * in0
@@ -359,8 +381,8 @@
 
     def lin_norm():
         total = ysend[...]
+        copies["all", 9].wait_recv()
         for step in range(n_head - 1):
-            copies["sums", step].wait_recv()
             total += yrecv[step]
         count = heads * size * n_head
         rscale_row = lax.rsqrt(total[0:1, :] / count + NORM_EPS)
@@ -384,16 +406,22 @@
             y0, y1 = jnp.where(first, own, other), jnp.where(first, other, own)
             p0, p1 = pass_rows(j)
             x0b[j] = y1
-            rsend[j] = (y0 + p0 * y1).astype(BF16)
-        copies["rnear"].start()
-        copies["rfar"].start()
+            comb[j] = y0 + p0 * y1
+            rsend[j] = comb[j].astype(BF16)
+            copies["r", j].start()
+
+    def back_relay():
+        for j in range(half):
+            copies["r", j].wait_recv()
+            both = pprod[0, pl.ds(2 * k + j, 1), :]
+            qsend[j] = (comb[j] + both * rnear[j].astype(F32)).astype(BF16)
+            copies["q", j].start()
 
     def back_get():
-        for name in ("rnear", "rfar", "pprev"):
-            copies[name].wait_recv()
         for j in range(half):
+            copies["q", j].wait_recv()
             p0, p1 = pass_rows(j)
-            out1 = rnear[j].astype(F32) + pprod[1, pl.ds(2 * k + j, 1), :] * rfar[j].astype(F32)
+            out1 = rfar[j].astype(F32)
             out0 = x0b[j] + p1 * out1
             back[2 * k + j] = jnp.where(first, out0, out1).astype(BF16)
             osend[j] = jnp.where(first, out1, out0).astype(BF16)
@@ -418,61 +446,65 @@
     enter_kernel()
     send_closing()
     load_kv()
-    send_own(0)
+    send_first(0)
     load_qd()
     send_qd(0)
     send_qd(1)
+    send_qd(2)
     local_lin()
     state_send()
+    send_first(1)
     send_own(1)
-    send_qd(2)
+    send_qd(3)
     local_soft()
+    state_relay()
     relay(0)
     send_own(2)
-    state_relay()
-    send_qd(3)
     relay(1)
     send_own(3)
     qrelay(0)
     qrelay(1)
     qrelay(2)
+    qrelay(3)
     state_get()
+    lin_raw()
+    relay_core(0)
     relay(2)
-    qrelay(3)
-    relay_core(0)
-    lin_raw()
-    relay(3)
-    relay_core(1)
     soft(0)
     qrelay_core(0)
     qrelay_core(1)
+    relay_core(1)
+    relay(3)
+    lin_norm()
+    soft(1)
+    back_send()
+    qrelay_core(2)
     relay_core(2)
-    soft(1)
-    qrelay_core(2)
-    lin_norm()
+    lin_local_grads()
+    finish(0)
+    finish(1)
+    soft(2)
     relay_core(3)
-    soft(2)
-    back_send()
     qrelay_core(3)
-    soft(3)
     later_mask()
     soft_grad(0)
-    finish(0)
+    back_relay()
+    soft(3)
     finish(4)
     finish(5)
-    lin_local_grads()
-    finish(1)
     soft_grad(1)
+    back_get()
     soft_grad(2)
-    back_get()
+    lin_grads()
+    finish(2)
+    finish(3)
     soft_grad(3)
     finish(6)
     finish(7)
-    lin_grads()
-    finish(2)
-    finish(3)
-    for copy in copies.values():
-        copy.wait_send()
+    for kind in range(14):
+        copies["all", kind].wait_send()
+    for name, _, _, _ in lin:
+        copies[name].wait_send()
 
 
 def write_out(*refs):
@@ -514,7 +546,7 @@
         vmem((heads, size, size), F32),
         vmem(half, F32),
         vmem((2, 8, size), F32),
-        vmem((2, 8, size), F32),
+        vmem((1, 8, size), F32),
         vmem(half, F32),
         vmem(half, F32),
         vmem(half, BF16),
@@ -534,22 +566,26 @@
         vmem(half, BF16),
         vmem(half, BF16),
         vmem(half, BF16),
+        vmem(half, BF16),
         vmem((heads, size, size), BF16),
         vmem(square, F32),
         vmem(square, F32),
         vmem((8,) + flat, F32),
         dma((8,)),
         dma((3,)),
+        dma((1,)),
+        dma((4,)),
         dma((4, heads)),
+        dma((4,)),
         dma((4, heads)),
-        dma((4, heads)),
-        dma((4, heads)),
-        dma((SPAN, heads)),
-        dma((SPAN, heads)),
-        dma((10,)),
-        dma((10,)),
-        dma((n_head,)),
-        dma((n_head,)),
+        dma((1,)),
+        dma((heads,)),
+        dma((5,)),
+        dma((5,)),
+        dma((4,)),
+        dma((4, heads // 2)),
+        dma((1,)),
+        dma((1,)),
     ]
     results = pl.pallas_call(
         functools.partial(kernel, n_ctx, n_head, heads, tok, size),

time: 46.3 us -> 43.8 us (0.946)
  Pallas kernels: 45.5 us -> 43 us
    pallas_call x1, Pallas kernels: 44.4 us -> 42 us  [shards(): pl.pallas_call(functools.partial(kernel, n_ctx, n_head, heads, tok, size)...]
where the time goes in v3:
time: 43.8 us; the launch traced here: 43.7 us
  Pallas kernels  43 us (98%)
  between operations  0.65 us (1%)
    pallas_call x1, Pallas kernels, shards(): pl.pallas_call(functools.partial(kernel, n_ctx, n_head, heads, tok, size)...  42 us
    pallas_call x1, Pallas kernels, shards(): pl.pallas_call(write_out, out_shape=[jax.ShapeDtypeStruct(flat, BF16)] *...  1.03 us

profile of v3, /device:TPU:1, one launch (start us, length us, event | category | flops | bytes accessed | tf_op | source)
XLA Modules:
  0.0 43.7 jit_solution(15027694347678958536)
XLA Ops:
  0.6 42.0 %shard_map.170 = (bf16[512,128]{1,0:T(8,128)(2,1)S(1)}, bf16[512,128]{1,0:T(8,128)(2,1)S(1)}, bf16[512,128]{1,0:T(8,128)(2,1)S(1)}, bf16[512,128]{1,0:T(8,128)(2...) custom-call(bf16[512,128]{1,0:T(8,128)(2,1)} %bitcast.17, ...), custom_call_target="tpu_custom_call" | custom-call | tf_op jit(solution)/shard_map/pallas_call | solution.py:590
  42.6 1.0 %shard_map.171 = (bf16[512,128]{1,0:T(8,128)(2,1)}, bf16[512,128]{1,0:T(8,128)(2,1)}, bf16[512,128]{1,0:T(8,128)(2,1)}, bf16[512,128]{1,0:T(8,128)(2,1)}, bf16[5...) custom-call(bf16[512,128]{1,0:T(8,128)(2,1)S(1)} %get-tuple-element.24.refs_, ...), custom_call_target="tpu_custom_call" | custom-call | tf_op jit(solution)/shard_map/pallas_call | solution.py:600

commit v4 on v3

--- a/solution.py
+++ b/solution.py
@@ -375,7 +375,6 @@
             crossed += head_of(LC, h) * ngv[h : h + 1, :] * value
         ysend[0:1, :] = jnp.sum(jnp.transpose(squares), axis=0, keepdims=True)
         ysend[1:2, :] = jnp.sum(jnp.transpose(crossed), axis=0, keepdims=True)
-        ysend[2:, :] = jnp.zeros((6, tok), F32)
         for step in range(n_head - 1):
             copies["sums", step].start()
 
@@ -493,12 +492,12 @@
     finish(4)
     finish(5)
     soft_grad(1)
+    soft_grad(2)
     back_get()
-    soft_grad(2)
+    soft_grad(3)
     lin_grads()
     finish(2)
     finish(3)
-    soft_grad(3)
     finish(6)
     finish(7)
     for kind in range(14):
@@ -555,8 +554,8 @@
         vmem(half, BF16),
         vmem(half, BF16),
         vmem((heads, size, size), BF16),
-        vmem((8, tok), F32),
-        vmem((n_head, 8, tok), F32),
+        vmem((2, tok), F32),
+        vmem((n_head, 2, tok), F32),
         vmem((heads, tok, tok), BF16),
         vmem(square, F32),
         vmem(square, BF16),

time: 43.8 us -> 43.4 us (level)
  no operation moved by 1% of the time
where the time goes in v4:
time: 43.4 us; the launch traced here: 43.3 us
  Pallas kernels  42.6 us (98%)
  between operations  0.65 us (1%)
    pallas_call x1, Pallas kernels, shards(): pl.pallas_call(functools.partial(kernel, n_ctx, n_head, heads, tok, size)...  41.6 us
    pallas_call x1, Pallas kernels, shards(): pl.pallas_call(write_out, out_shape=[jax.ShapeDtypeStruct(flat, BF16)] *...  1.03 us

profile of v4, /device:TPU:1, one launch (start us, length us, event | category | flops | bytes accessed | tf_op | source)
XLA Modules:
  0.0 43.3 jit_solution(10775284359045554789)
XLA Ops:
  0.6 41.6 %shard_map.170 = (bf16[512,128]{1,0:T(8,128)(2,1)S(1)}, bf16[512,128]{1,0:T(8,128)(2,1)S(1)}, bf16[512,128]{1,0:T(8,128)(2,1)S(1)}, bf16[512,128]{1,0:T(8,128)(2...) custom-call(bf16[512,128]{1,0:T(8,128)(2,1)} %bitcast.17, ...), custom_call_target="tpu_custom_call" | custom-call | tf_op jit(solution)/shard_map/pallas_call | solution.py:589
  42.2 1.0 %shard_map.171 = (bf16[512,128]{1,0:T(8,128)(2,1)}, bf16[512,128]{1,0:T(8,128)(2,1)}, bf16[512,128]{1,0:T(8,128)(2,1)}, bf16[512,128]{1,0:T(8,128)(2,1)}, bf16[5...) custom-call(bf16[512,128]{1,0:T(8,128)(2,1)S(1)} %get-tuple-element.24.refs_, ...), custom_call_target="tpu_custom_call" | custom-call | tf_op jit(solution)/shard_map/pallas_call | solution.py:599

commit v5 on v4

--- a/solution.py
+++ b/solution.py
@@ -247,7 +247,7 @@
         delta = jnp.sum(cot.astype(F32) * out, axis=1, keepdims=True)
         lane = lax.broadcasted_iota(jnp.int32, (tok, tok), 1)
         figures = jnp.where(lane == 0, top + jnp.log(total), jnp.where(lane == 1, delta, mask[1]))
-        stats[h, 0] = jnp.transpose(figures)[:8, :]
+        stats[h, 0] = jnp.transpose(figures)[:4, :]
         for i in range(SPAN):
             copies["stats", h, i].start()
         slopes = inv_root * (expo * inverse) * (dot_nt(cot, values) - delta)
@@ -541,7 +541,7 @@
         vmem(square, F32),
         vmem(square, F32),
         vmem(wide, BF16),
-        vmem((heads, SPAN + 1, 8, tok), F32),
+        vmem((heads, SPAN + 1, 4, tok), F32),
         vmem((heads, size, size), F32),
         vmem(half, F32),
         vmem((2, 8, size), F32),

time: 43.4 us -> 43.4 us (level)
  no operation moved by 1% of the time
where the time goes in v5:
time: 43.4 us; the launch traced here: 43.3 us
  Pallas kernels  42.6 us (98%)
  between operations  0.65 us (1%)
    pallas_call x1, Pallas kernels, shards(): pl.pallas_call(functools.partial(kernel, n_ctx, n_head, heads, tok, size)...  41.6 us
    pallas_call x1, Pallas kernels, shards(): pl.pallas_call(write_out, out_shape=[jax.ShapeDtypeStruct(flat, BF16)] *...  1.03 us

profile of v5, /device:TPU:1, one launch (start us, length us, event | category | flops | bytes accessed | tf_op | source)
XLA Modules:
  0.0 43.3 jit_solution(13899021092546647410)
XLA Ops:
  0.6 41.6 %shard_map.170 = (bf16[512,128]{1,0:T(8,128)(2,1)S(1)}, bf16[512,128]{1,0:T(8,128)(2,1)S(1)}, bf16[512,128]{1,0:T(8,128)(2,1)S(1)}, bf16[512,128]{1,0:T(8,128)(2...) custom-call(bf16[512,128]{1,0:T(8,128)(2,1)} %bitcast.17, ...), custom_call_target="tpu_custom_call" | custom-call | tf_op jit(solution)/shard_map/pallas_call | solution.py:589
  42.2 1.0 %shard_map.171 = (bf16[512,128]{1,0:T(8,128)(2,1)}, bf16[512,128]{1,0:T(8,128)(2,1)}, bf16[512,128]{1,0:T(8,128)(2,1)}, bf16[512,128]{1,0:T(8,128)(2,1)}, bf16[5...) custom-call(bf16[512,128]{1,0:T(8,128)(2,1)S(1)} %get-tuple-element.24.refs_, ...), custom_call_target="tpu_custom_call" | custom-call | tf_op jit(solution)/shard_map/pallas_call | solution.py:599
